TPU v7x, 32 devices: a whole 2x2x4 slice. The times are simulated.
32 devices in a mesh: grp: 2 (over core), fsdp: 16 (over z, y, x).
Axes of the slice: x: 2, y: 2, z: 4, core: 2. Of those that a mesh axis runs over, the one named last changes fastest.
Arguments:
- tokens: bfloat16 [32768, 1024], P(('grp', 'fsdp')), may hold values from -6 to 6
- cotangent: bfloat16 [32768, 1024], P(('grp', 'fsdp')), may hold values from -6 to 6
- segment_ids: int32 [32768], P(('grp', 'fsdp')), may hold values from 0 to 127, as said below
- group_counts: int32 [2], replicated, may hold values from 1000 to 4999
- qkv_weight: float32 [1024, 3072], P('fsdp'), may hold values from -0.1875 to 0.1875
- out_weight: float32 [1024, 1024], P('fsdp'), may hold values from -0.75 to 0.75
- up_weight: float32 [1024, 4096], P('fsdp'), may hold values from -0.1875 to 0.1875
- down_weight: float32 [4096, 1024], P('fsdp'), may hold values from -0.09375 to 0.09375
- small_params: float32 [12288], P('fsdp')
- qkv_first: float32 [1024, 3072], P('fsdp'), may hold values from -0.00048828125 to 0.00048828125
- out_first: float32 [1024, 1024], P('fsdp'), may hold values from -0.00048828125 to 0.00048828125
- up_first: float32 [1024, 4096], P('fsdp'), may hold values from -0.00048828125 to 0.00048828125
- down_first: float32 [4096, 1024], P('fsdp'), may hold values from -0.00048828125 to 0.00048828125
- small_first: float32 [12288], P('fsdp'), may hold values from -0.00048828125 to 0.00048828125
- qkv_second: float32 [1024, 3072], P('fsdp'), may hold values from 7.947286e-11 to 3.1789144e-10
- out_second: float32 [1024, 1024], P('fsdp'), may hold values from 7.947286e-11 to 3.1789144e-10
- up_second: float32 [1024, 4096], P('fsdp'), may hold values from 7.947286e-11 to 3.1789144e-10
- down_second: float32 [4096, 1024], P('fsdp'), may hold values from 7.947286e-11 to 3.1789144e-10
- small_second: float32 [12288], P('fsdp'), may hold values from 7.947286e-11 to 3.1789144e-10
Outputs:
- block_output: bfloat16 [32768, 1024], P(('grp', 'fsdp'))
- tokens_grad: bfloat16 [32768, 1024], P(('grp', 'fsdp'))
- new_qkv_weight: float32 [1024, 3072], P('fsdp')
- new_out_weight: float32 [1024, 1024], P('fsdp')
- new_up_weight: float32 [1024, 4096], P('fsdp')
- new_down_weight: float32 [4096, 1024], P('fsdp')
- new_small_params: float32 [12288], P('fsdp')
- new_qkv_first: float32 [1024, 3072], P('fsdp')
- new_out_first: float32 [1024, 1024], P('fsdp')
- new_up_first: float32 [1024, 4096], P('fsdp')
- new_down_first: float32 [4096, 1024], P('fsdp')
- new_small_first: float32 [12288], P('fsdp')
- new_qkv_second: float32 [1024, 3072], P('fsdp')
- new_out_second: float32 [1024, 1024], P('fsdp')
- new_up_second: float32 [1024, 4096], P('fsdp')
- new_down_second: float32 [4096, 1024], P('fsdp')
- new_small_second: float32 [12288], P('fsdp')
- grad_norm_sq: float32 [], replicated
Inputs may be any that keep to these rules, and one draw needn't show every extreme that they name: `segment_ids`: within each device's 1024 tokens the numbers start at 0, never fall, and equal numbers form one crop. On devices of the global group crops hold 40 to 50 tokens and the first holds 50; on the local group 8 to 10 and the first 10; a device's last crop may be cut short. The first device of the local group has crops of 8 tokens after its first.
All inputs are finite; a program needn't handle non-finite values.
Results may differ from a plain program's by a relative error of at most 0.017.
Values may be sent and summed in bfloat16 or wider, within the bound.
No kernel may reach another device: no remote copies, remote signals or barrier semaphores. Data moves between devices by JAX's collectives and lax.ppermute only.
A program may use at most 256 MiB of HBM per device.

v0:
```python
import jax
import jax.numpy as jnp
from jax import lax
from jax.sharding import PartitionSpec as P

HD = 64
STEP = 10


EPS_NORM = 1e-06
CLIP = 1.0
RATE = 0.04
RATE_SMALL = 0.25
DECAY = 0.05
BETA_ONE = 0.9
BETA_TWO = 0.999
EPS_ADAM = 1e-08
MARGIN = 64


def layer_norm(x, gain, bias):
    mean = jnp.mean(x, -1, keepdims=True)
    centred = x - mean
    var = jnp.mean(centred * centred, -1, keepdims=True)
    return centred * lax.rsqrt(var + EPS_NORM) * gain + bias


def unpack(small, width, hidden):
    pieces = [small[i * width : (i + 1) * width] for i in range(7)]
    return pieces + [small[7 * width : 7 * width + hidden], small[7 * width + hidden :]]


def window_stack(array, first, group, tile):
    span = group * tile + 2 * MARGIN
    piece = lax.dynamic_slice_in_dim(array, first, span, 0)
    return jnp.stack([piece[j * tile : j * tile + tile + 2 * MARGIN] for j in range(group)])


def masked_scores(q_grp, key_win, seg_grp, seg_win, heads):
    group, tile, width = q_grp.shape
    span = key_win.shape[1]
    head_size = width // heads
    scores = jnp.einsum(
        "bqhd,bkhd->bhqk",
        q_grp.reshape(group, tile, heads, head_size),
        key_win.reshape(group, span, heads, head_size),
        preferred_element_type=jnp.float32,
    ) * head_size ** (-0.5)
    same = seg_grp[:, :, None] == seg_win[:, None, :]
    return jnp.where(same[:, None], scores, -1e30)


def adam(weight, first, second, grad, decay, rate):
    first = BETA_ONE * first + (1.0 - BETA_ONE) * grad
    second = BETA_TWO * second + (1.0 - BETA_TWO) * grad * grad
    step_size = (
        first / (1.0 - BETA_ONE**STEP) / (jnp.sqrt(second / (1.0 - BETA_TWO**STEP)) + EPS_ADAM)
    )
    return (weight - rate * (step_size + decay * weight), first, second)


def shards(
    tokens,
    cotangent,
    segment_ids,
    group_counts,
    qkv_weight,
    out_weight,
    up_weight,
    down_weight,
    small_params,
    qkv_first,
    out_first,
    up_first,
    down_first,
    small_first,
    qkv_second,
    out_second,
    up_second,
    down_second,
    small_second,
):
    half = jnp.bfloat16
    width = tokens.shape[1]
    hidden = up_weight.shape[1]
    heads = width // HD
    head_size = HD
    rows = tokens.shape[0]
    tile = min(128, rows)
    ntiles = rows // tile
    group = min(4, ntiles)
    nsteps = ntiles // group
    span = tile + 2 * MARGIN
    gathered = (
        lax.all_gather(qkv_weight.astype(half), "fsdp", axis=0, tiled=True),
        lax.all_gather(out_weight.astype(half), "fsdp", axis=0, tiled=True),
        lax.all_gather(up_weight.astype(half), "fsdp", axis=0, tiled=True),
        lax.all_gather(down_weight.astype(half), "fsdp", axis=0, tiled=True),
        lax.all_gather(small_params.astype(half), "fsdp", axis=0, tiled=True),
    )
    qkv_full, out_full, up_full, down_full, small_low = gathered
    small_full = small_low.astype(jnp.float32)
    gain_one, bias_one, bias_query, bias_value, bias_out, gain_two, bias_two, bias_up, bias_down = (
        unpack(small_full, width, hidden)
    )
    inputs = tokens.astype(jnp.float32)
    normed_one_low = layer_norm(inputs, gain_one, bias_one).astype(half)
    qkv_bias = jnp.concatenate([bias_query, jnp.zeros_like(bias_query), bias_value])
    project = (
        jnp.dot(normed_one_low, qkv_full, preferred_element_type=jnp.float32) + qkv_bias
    ).astype(half)
    queries = project[:, :width]
    keys_pad = jnp.pad(project[:, width : 2 * width], ((MARGIN, MARGIN), (0, 0)))
    values_pad = jnp.pad(project[:, 2 * width :], ((MARGIN, MARGIN), (0, 0)))
    seg_pad = jnp.pad(segment_ids, (MARGIN, MARGIN), constant_values=-1)
    query_groups = queries.reshape(nsteps, group, tile, width)
    seg_groups = segment_ids.reshape(nsteps, group, tile)
    step_index = jnp.arange(nsteps, dtype=jnp.int32)

    def forward_step(item):
        index, q_grp, seg_grp = item
        first = index * (group * tile)
        key_win = window_stack(keys_pad, first, group, tile)
        value_win = window_stack(values_pad, first, group, tile).reshape(
            group, span, heads, head_size
        )
        seg_win = window_stack(seg_pad, first, group, tile)
        scores = masked_scores(q_grp, key_win, seg_grp, seg_win, heads)
        top = jnp.max(scores, -1, keepdims=True)
        expo = jnp.exp(scores - top)
        total = jnp.sum(expo, -1, keepdims=True)
        probs = expo / total
        mixed = jnp.einsum(
            "bhqk,bkhd->bqhd", probs.astype(half), value_win, preferred_element_type=jnp.float32
        )
        return (mixed.reshape(group, tile, width).astype(half), top + jnp.log(total))

    att_groups, lse_groups = lax.map(forward_step, (step_index, query_groups, seg_groups))
    att_low = att_groups.reshape(rows, width)
    middle = inputs + jnp.dot(att_low, out_full, preferred_element_type=jnp.float32) + bias_out
    normed_two_low = layer_norm(middle, gain_two, bias_two).astype(half)
    pre_act = jnp.dot(normed_two_low, up_full, preferred_element_type=jnp.float32) + bias_up
    act_low = jax.nn.gelu(pre_act).astype(half)
    output = middle + jnp.dot(act_low, down_full, preferred_element_type=jnp.float32) + bias_down
    block_output = output.astype(half)
    qkv_back, out_back, up_back, down_back = (qkv_full, out_full, up_full, down_full)
    grad_out = cotangent.astype(jnp.float32)
    grad_bias_down = jnp.sum(grad_out, 0)
    grad_down = jnp.einsum("tf,td->fd", act_low, cotangent, preferred_element_type=jnp.float32)
    grad_act = jnp.einsum("td,fd->tf", cotangent, down_back, preferred_element_type=jnp.float32)
    grad_pre_low = jax.vjp(jax.nn.gelu, pre_act)[1](grad_act)[0].astype(half)
    grad_bias_up = jnp.sum(grad_pre_low.astype(jnp.float32), 0)
    grad_up = jnp.einsum(
        "td,tf->df", normed_two_low, grad_pre_low, preferred_element_type=jnp.float32
    )
    grad_normed_two = jnp.einsum(
        "tf,df->td", grad_pre_low, up_back, preferred_element_type=jnp.float32
    )
    grad_mid, grad_gain_two, grad_bias_two = jax.vjp(layer_norm, middle, gain_two, bias_two)[1](
        grad_normed_two
    )
    grad_mid = grad_out + grad_mid
    grad_mid_low = grad_mid.astype(half)
    grad_bias_out = jnp.sum(grad_mid_low.astype(jnp.float32), 0)
    grad_out_weight = jnp.einsum(
        "td,te->de", att_low, grad_mid_low, preferred_element_type=jnp.float32
    )
    grad_att_low = jnp.einsum(
        "te,de->td", grad_mid_low, out_back, preferred_element_type=jnp.float32
    ).astype(half)

    def backward_step(carry, item):
        grad_keys, grad_values = carry
        index, q_grp, seg_grp, do_grp, lse_grp = item
        first = index * (group * tile)
        key_win = window_stack(keys_pad, first, group, tile)
        value_win = window_stack(values_pad, first, group, tile).reshape(
            group, span, heads, head_size
        )
        seg_win = window_stack(seg_pad, first, group, tile)
        scores = masked_scores(q_grp, key_win, seg_grp, seg_win, heads)
        probs = jnp.exp(scores - lse_grp)
        do_heads = do_grp.reshape(group, tile, heads, head_size)
        grad_probs = jnp.einsum(
            "bqhd,bkhd->bhqk", do_heads, value_win, preferred_element_type=jnp.float32
        )
        grad_scores = (
            probs * (grad_probs - jnp.sum(probs * grad_probs, -1, keepdims=True))
        ).astype(half)
        scale = head_size ** (-0.5)
        grad_q = (
            jnp.einsum(
                "bhqk,bkhd->bqhd",
                grad_scores,
                key_win.reshape(group, span, heads, head_size),
                preferred_element_type=jnp.float32,
            )
            * scale
        )
        key_part = (
            jnp.einsum(
                "bhqk,bqhd->bkhd",
                grad_scores,
                q_grp.reshape(group, tile, heads, head_size),
                preferred_element_type=jnp.float32,
            )
            * scale
        ).reshape(group, span, width)
        value_part = jnp.einsum(
            "bhqk,bqhd->bkhd", probs.astype(half), do_heads, preferred_element_type=jnp.float32
        ).reshape(group, span, width)
        for j in range(group):
            place = first + j * tile
            grad_keys = lax.dynamic_update_slice_in_dim(
                grad_keys,
                lax.dynamic_slice_in_dim(grad_keys, place, span, 0) + key_part[j],
                place,
                0,
            )
            grad_values = lax.dynamic_update_slice_in_dim(
                grad_values,
                lax.dynamic_slice_in_dim(grad_values, place, span, 0) + value_part[j],
                place,
                0,
            )
        return ((grad_keys, grad_values), grad_q.reshape(group, tile, width))

    empty = jnp.zeros((rows + 2 * MARGIN, width), jnp.float32)
    (grad_keys_pad, grad_values_pad), grad_q_groups = lax.scan(
        backward_step,
        (empty, empty),
        (
            step_index,
            query_groups,
            seg_groups,
            grad_att_low.reshape(nsteps, group, tile, width),
            lse_groups,
        ),
    )
    grad_keys = grad_keys_pad[MARGIN : MARGIN + rows]
    grad_values = grad_values_pad[MARGIN : MARGIN + rows]
    grad_project_low = jnp.concatenate(
        [grad_q_groups.reshape(rows, width), grad_keys, grad_values], 1
    ).astype(half)
    grad_project = grad_project_low.astype(jnp.float32)
    grad_bias_query = jnp.sum(grad_project[:, :width], 0)
    grad_bias_value = jnp.sum(grad_project[:, 2 * width :], 0)
    grad_qkv = jnp.einsum(
        "td,te->de", normed_one_low, grad_project_low, preferred_element_type=jnp.float32
    )
    grad_normed_one = jnp.einsum(
        "te,de->td", grad_project_low, qkv_back, preferred_element_type=jnp.float32
    )
    grad_in, grad_gain_one, grad_bias_one = jax.vjp(layer_norm, inputs, gain_one, bias_one)[1](
        grad_normed_one
    )
    tokens_grad = (grad_mid + grad_in).astype(half)
    grad_small = jnp.concatenate(
        [
            grad_gain_one,
            grad_bias_one,
            grad_bias_query,
            grad_bias_value,
            grad_bias_out,
            grad_gain_two,
            grad_bias_two,
            grad_bias_up,
            grad_bias_down,
        ]
    )
    counts = group_counts.astype(jnp.float32)
    share = counts / jnp.sum(counts)
    is_local = lax.axis_index("grp") >= lax.axis_size("grp") // 2
    mine = jnp.where(is_local, share[1], share[0])
    terms = (grad_qkv, grad_out_weight, grad_up, grad_down, grad_small)
    olds = (qkv_weight, out_weight, up_weight, down_weight, small_params)
    firsts = (qkv_first, out_first, up_first, down_first, small_first)
    seconds = (qkv_second, out_second, up_second, down_second, small_second)
    decays = (DECAY, DECAY, DECAY, DECAY, 0.0)
    rates = (RATE, RATE, RATE, RATE, RATE_SMALL)
    owned = (
        lax.psum_scatter(terms[0], "fsdp", scatter_dimension=0, tiled=True),
        lax.psum_scatter(terms[1], "fsdp", scatter_dimension=0, tiled=True),
        lax.psum_scatter(terms[2], "fsdp", scatter_dimension=0, tiled=True),
        lax.psum_scatter(terms[3], "fsdp", scatter_dimension=0, tiled=True),
        lax.psum_scatter(terms[4], "fsdp", scatter_dimension=0, tiled=True),
    )
    owned = tuple((mine * piece for piece in owned))
    merged = (
        lax.psum(owned[0].astype(jnp.bfloat16), "grp").astype(jnp.float32),
        lax.psum(owned[1].astype(jnp.bfloat16), "grp").astype(jnp.float32),
        lax.psum(owned[2].astype(jnp.bfloat16), "grp").astype(jnp.float32),
        lax.psum(owned[3].astype(jnp.bfloat16), "grp").astype(jnp.float32),
        lax.psum(owned[4].astype(jnp.bfloat16), "grp").astype(jnp.float32),
    )
    local_sq = sum((jnp.sum(piece * piece) for piece in merged))
    total_sq = lax.psum(local_sq, "fsdp")
    scale = jnp.minimum(1.0, CLIP * lax.rsqrt(total_sq))
    results = [
        adam(w, m, v, g * scale, dc, rt)
        for w, m, v, g, dc, rt in zip(olds, firsts, seconds, merged, decays, rates)
    ]
    return (
        block_output,
        tokens_grad,
        results[0][0],
        results[1][0],
        results[2][0],
        results[3][0],
        results[4][0],
        results[0][1],
        results[1][1],
        results[2][1],
        results[3][1],
        results[4][1],
        results[0][2],
        results[1][2],
        results[2][2],
        results[3][2],
        results[4][2],
        total_sq,
    )


def solution(mesh):
    return jax.shard_map(
        shards,
        mesh=mesh,
        in_specs=(
            P(("grp", "fsdp"), None),
            P(("grp", "fsdp"), None),
            P(("grp", "fsdp")),
            P(),
            P("fsdp", None),
            P("fsdp", None),
            P("fsdp", None),
            P("fsdp", None),
            P("fsdp"),
            P("fsdp", None),
            P("fsdp", None),
            P("fsdp", None),
            P("fsdp", None),
            P("fsdp"),
            P("fsdp", None),
            P("fsdp", None),
            P("fsdp", None),
            P("fsdp", None),
            P("fsdp"),
        ),
        out_specs=(
            P(("grp", "fsdp"), None),
            P(("grp", "fsdp"), None),
            P("fsdp", None),
            P("fsdp", None),
            P("fsdp", None),
            P("fsdp", None),
            P("fsdp"),
            P("fsdp", None),
            P("fsdp", None),
            P("fsdp", None),
            P("fsdp", None),
            P("fsdp"),
            P("fsdp", None),
            P("fsdp", None),
            P("fsdp", None),
            P("fsdp", None),
            P("fsdp"),
            P(),
        ),
        check_vma=False,
    )
```

profile of v0, /device:TPU:0, one launch (start us, length us, event | category | flops | bytes accessed | tf_op | source)
XLA Modules:
  0.0 1663.4 jit_solution(10636361673819281321)
XLA Ops:
  14.2 43.1 %all-gather = bf16[16,1,768]{2,1,0:T(2,128)(2,1)S(1)} all-gather(bf16[1,1,768]{2,1,0:T(2,128)(2,1)S(1)} %reshape.273), channel_id=1, replica_groups=mesh['grp'=2,'fsdp'=16] {'fsdp'}, dimensions={0}, use_global_device_ids=true | all-gather | bytes 26112 | tf_op jit(solution)/shard_map/all_gather | solution.py:99
  67.2 41.3 %all-gather.6.cloned.1.call-done = bf16[1024,3072]{1,0:T(8,128)(2,1)} async-done(((bf16[64,3072]{1,0:T(8,128)(2,1)}), bf16[1024,3072]{1,0:T(8,128)(2,1)}) %all-gather.6.cloned.1.call-update) | async-done | bytes 6291472 | tf_op jit(solution)/shard_map/all_gather | solution.py:95
  108.5 10.3 add_convert_fusion
  137.6 36.0 %while.28 = (s32[]{:T(128)}, bf16[2,4,128,1024]{3,2,1,0:T(8,128)(2,1)}, f32[2,4,16,128,1]{3,2,1,4,0:T(8,128)S(1)}, s32[2]{0:T(128)S(1)}, bf16[1152,1024]{0,1:T(8...) while((s32[]{:T(128)}, ...), condition=%wide.region_5.6_spmd, body=%wide.region_2.5_spmd.sunk | while | flops 568978432 | bytes 46955808 | solution.py:138
  173.6 5.7 fusion.123
  181.8 103.9 %all-gather.10.cloned.1.call-done = bf16[1024,4096]{1,0:T(8,128)(2,1)} async-done(((bf16[64,4096]{1,0:T(8,128)(2,1)}), bf16[1024,4096]{1,0:T(8,128)(2,1)}) %all-gather.10.cloned.1.call-update) | async-done | bytes 8388624 | tf_op jit(solution)/shard_map/all_gather | solution.py:97
  285.7 17.2 %fusion.101 = f32[1024,4096]{1,0:T(8,128)} fusion(bf16[1024,4096]{1,0:T(8,128)(2,1)} %all-gather.10.cloned.1.call-done, f32[1024,1024]{0,1:T(8,128)} %copy-done.5, f32[1024]{0:T(1024)S(1)} %copy-done.61, f32[1024]{0:T(1024)S(1)} %copy-done.45, f32[1024]{0:T(1024)S(1)} %fusion.94, f32[1024]{0:T(1024)S(1)} %broadcast_multiply_fusion), kind=kOutput, calls=%fused_computation.218 | convolution fusion | flops 8595177472 | bytes 29376512 | tf_op jit(solution)/shard_map/dot_general | solution.py:142
  302.9 97.1 %all-gather.12.cloned.1.call-done = bf16[4096,1024]{1,0:T(8,128)(2,1)} async-done(((bf16[256,1024]{1,0:T(8,128)(2,1)}), bf16[4096,1024]{1,0:T(8,128)(2,1)}) %all-gather.12.cloned.1.call-update) | async-done | bytes 8388624 | tf_op jit(solution)/shard_map/all_gather | solution.py:98
  400.0 26.4 %convert_reduce_fusion = (f32[4096]{0:T(1024)}, bf16[1024,4096]{1,0:T(8,128)(2,1)}) fusion(f32[1024,4096]{1,0:T(8,128)} %fusion.101, f32[4096]{0:T(1024)S(1)} %copy-done.55, bf16[1024,1024]{1,0:T(8,128)(2,1)} %param.24, bf16[4096,1024]{1,0:T(8,128)(2,1)} %all-gather.12.cloned.1.call-done), kind=kOutput, calls=%fused_computation.109 | convolution fusion | flops 8686399488 | bytes 35684352 | tf_op jit(solution)/shard_map/td,fd->tf/dot_general | solution.py:150
  426.4 15.9 fusion.125
  462.5 5.9 convolution_convert_fusion
  473.4 98.1 %while.29 = (s32[]{:T(128)}, f32[1152,1024]{0,1:T(8,128)}, f32[1152,1024]{0,1:T(8,128)}, bf16[2,4,128,1024]{3,2,1,0:T(8,128)(2,1)}, s32[2]{0:T(128)S(1)}, /*inde...) while((s32[]{:T(128)}, f32[1152,1024]{0,1:T(8,128)}, ...), condition=%wide.region_12.13_spmd, body=%wide.region_10.12_spmd.sunk | while | flops 1387392000 | bytes 166067888 | solution.py:229
  585.0 11.4 fusion.95
  597.0 20.1 %fusion.102 = f32[4096,1024]{1,0:T(8,128)} fusion(bf16[1024,1024]{1,0:T(8,128)(2,1)} %param.24, f32[1024,4096]{1,0:T(8,128)} %fusion.101, f32[4096]{0:T(1024)S(1)} %copy-done.56), kind=kOutput, calls=%fused_computation.219 | convolution fusion | flops 8631877632 | bytes 35667968 | tf_op jit(solution)/shard_map/tf,td->fd/dot_general | solution.py:149
  617.9 16.9 %fusion.100 = f32[1024,4096]{1,0:T(8,128)} fusion(bf16[1024,4096]{1,0:T(8,128)(2,1)} %get-tuple-element.409, f32[1024,1024]{0,1:T(8,128)} %copy-done.5, f32[1024]{0:T(1024)S(1)} %copy-done.62, f32[1024]{0:T(1024)S(1)} %copy-done.46, f32[1024]{0:T(1024)S(1)} %copy-done.50, f32[1024]{0:T(1024)S(1)} %copy-done.42), kind=kOutput, calls=%fused_computation.217 | convolution fusion | flops 8595177472 | bytes 29376512 | tf_op jit(solution)/shard_map/td,tf->df/dot_general | solution.py:153
  639.9 17.6 %add_convert_fusion.2 = bf16[1024,1024]{0,1:T(8,128)(2,1)} fusion(f32[1024,1024]{0,1:T(8,128)} %copy-done.5, f32[1024]{0:T(1024)S(1)} %copy-done.60, bf16[4096,1024]{1,0:T(8,128)(2,1)} %all-gather.12.cloned.1.call-done, f32[1024,4096]{1,0:T(8,128)} %fusion.101, f32[4096]{0:T(1024)S(1)} %copy-done.56), kind=kOutput, calls=%fused_computation.140 | convolution fusion | flops 8635023360 | bytes 31477760 | tf_op jit(solution)/shard_map/dot_general | solution.py:144
  661.5 12.1 fusion.124
  673.6 5.4 copy.88
  689.0 109.7 %reduce-scatter.5.cloned.1.call-done = f32[64,3072]{1,0:T(8,128)} async-done(((f32[1024,3072]{1,0:T(8,128)}), f32[64,3072]{1,0:T(8,128)}) %reduce-scatter.5.cloned.1.call-update) | async-done | bytes 786448 | tf_op jit(solution)/shard_map/reduce_scatter | solution.py:282
  800.7 346.5 %reduce-scatter.11.cloned.1.call-done = f32[256,1024]{1,0:T(8,128)} async-done(((f32[4096,1024]{1,0:T(8,128)}), f32[256,1024]{1,0:T(8,128)}) %reduce-scatter.11.cloned.1.call-update) | async-done | bytes 1048592 | tf_op jit(solution)/shard_map/reduce_scatter | solution.py:285
  1149.3 352.3 %reduce-scatter.9.cloned.1.call-done = f32[64,4096]{1,0:T(8,128)} async-done(((f32[1024,4096]{1,0:T(8,128)}), f32[64,4096]{1,0:T(8,128)}) %reduce-scatter.9.cloned.1.call-update) | async-done | bytes 1048592 | tf_op jit(solution)/shard_map/reduce_scatter | solution.py:284
  1503.8 6.5 convert_reduce_fusion.2
  1510.3 79.4 %all-reduce.3 = f32[12288]{0:T(1024)S(1)} all-reduce(f32[12288]{0:T(1024)S(1)} %constant_dynamic-update-slice_fusion.10), channel_id=6, replica_groups=mesh['grp'=2,'fsdp'=16] {'fsdp'}, use_global_device_ids=true, to_apply=%region_37.38.clone | all-reduce | flops 12288 | bytes 98304
  1607.3 37.2 %psum.47 = f32[]{:T(128)} all-reduce(f32[]{:T(128)S(6)} %add.375), channel_id=1, replica_groups=mesh['grp'=2,'fsdp'=16] {'fsdp'}, use_global_device_ids=true, to_apply=%region_40.41 | all-reduce | flops 1 | bytes 8 | tf_op jit(solution)/shard_map/psum | solution.py:297
  (344 shorter events, 256.8 us)
Async XLA Ops:
  7.2 101.3 %all-gather.6.cloned.1.call-start = ((), (), s32[]{:S(2)}) async-start(), calls=%async_computation.4 | async-start | bytes 6684672 | tf_op jit(solution)/shard_map/all_gather | solution.py:95
  9.3 164.3 %all-gather.8.cloned.1.call-start = ((), (), s32[]{:S(2)}) async-start(), calls=%async_computation.5 | async-start | bytes 2228224 | tf_op jit(solution)/shard_map/all_gather | solution.py:96
  11.0 274.7 %all-gather.10.cloned.1.call-start = ((), (), s32[]{:S(2)}) async-start(), calls=%async_computation.6 | async-start | bytes 8912896 | tf_op jit(solution)/shard_map/all_gather | solution.py:97
  13.1 386.8 %all-gather.12.cloned.1.call-start = ((), (), s32[]{:S(2)}) async-start(), calls=%async_computation.7 | async-start | bytes 8912896 | tf_op jit(solution)/shard_map/all_gather | solution.py:98
  14.1 673.3 %reduce-scatter.7.cloned.1.call-start = ((), (), s32[]{:S(2)}) async-start(), calls=%async_computation.9 | async-start | bytes 4456448 | tf_op jit(solution)/shard_map/reduce_scatter | solution.py:283
  179.3 106.4 %copy-start.45 = (f32[1024]{0:T(1024)S(1)}, f32[1024]{0:T(1024)}, u32[]{:S(2)}) copy-start(f32[1024]{0:T(1024)} %get-tuple-element.463) | copy-start | bytes 12292
  179.3 273.7 %copy-start.41 = (f32[1024]{0:T(1024)}, f32[1024]{0:T(1024)S(1)}, u32[]{:S(2)}) copy-start(f32[1024]{0:T(1024)S(1)} %broadcast_multiply_fusion) | copy-start | bytes 12292
  181.8 271.2 %copy-start.49 = (f32[1024]{0:T(1024)}, f32[1024]{0:T(1024)S(1)}, u32[]{:S(2)}) copy-start(f32[1024]{0:T(1024)S(1)} %fusion.94) | copy-start | bytes 12292
  285.7 114.2 %copy-start.55 = (f32[4096]{0:T(1024)S(1)}, f32[4096]{0:T(1024)}, u32[]{:S(2)}) copy-start(f32[4096]{0:T(1024)} %slice.256) | copy-start | bytes 49156
  462.5 336.3 %reduce-scatter.5.cloned.1.call-start = ((), (), s32[]{:S(2)}) async-start(), calls=%async_computation.8 | async-start | bytes 13369344 | tf_op jit(solution)/shard_map/reduce_scatter | solution.py:282
  596.3 550.8 %reduce-scatter.11.cloned.1.call-start = ((), (), s32[]{:S(2)}) async-start(), calls=%async_computation.11 | async-start | bytes 17825792 | tf_op jit(solution)/shard_map/reduce_scatter | solution.py:285
  617.2 884.4 %reduce-scatter.9.cloned.1.call-start = ((), (), s32[]{:S(2)}) async-start(), calls=%async_computation.10 | async-start | bytes 17825792 | tf_op jit(solution)/shard_map/reduce_scatter | solution.py:284
  634.9 958.0 %all-reduce.7.cloned.1.call-start = ((), (), s32[]{:S(2)}) async-start(), calls=%async_computation.12 | async-start | bytes 3145728 | tf_op jit(solution)/shard_map/psum | solution.py:290
  687.2 816.4 %copy-start.53 = (f32[1024]{0:T(1024)S(1)}, f32[1024]{0:T(1024)}, u32[]{:S(2)}) copy-start(f32[1024]{0:T(1024)} %get-tuple-element.410) | copy-start | bytes 12292
  687.3 816.4 %copy-start.54 = (f32[1024]{0:T(1024)S(1)}, f32[1024]{0:T(1024)}, u32[]{:S(2)}) copy-start(f32[1024]{0:T(1024)} %get-tuple-element.343) | copy-start | bytes 12292
  687.3 816.5 %copy-start.66 = (f32[1024]{0:T(1024)S(1)}, f32[1024]{0:T(1024)}, u32[]{:S(2)}) copy-start(f32[1024]{0:T(1024)} %get-tuple-element.477) | copy-start | bytes 12292
  687.3 816.5 %copy-start.57 = (f32[4096]{0:T(1024)S(1)}, f32[4096]{0:T(1024)}, u32[]{:S(2)}) copy-start(f32[4096]{0:T(1024)} %get-tuple-element.408) | copy-start | bytes 49156
  687.3 816.5 %copy-start.44 = (f32[1024]{0:T(1024)S(1)}, f32[1024]{0:T(1024)}, u32[]{:S(2)}) copy-start(f32[1024]{0:T(1024)} %copy-done.43) | copy-start | bytes 12292
  1510.2 135.0 %copy-start.59 = (f32[768]{0:T(1024)S(1)}, f32[768]{0:T(1024)}, u32[]{:S(2)}) copy-start(f32[768]{0:T(1024)} %param.31) | copy-start | bytes 9220
  1510.2 135.0 %copy-start.67 = (f32[768]{0:T(1024)S(1)}, f32[768]{0:T(1024)}, u32[]{:S(2)}) copy-start(f32[768]{0:T(1024)} %param.36) | copy-start | bytes 9220
  1510.3 135.0 %copy-start.68 = (f32[768]{0:T(1024)S(1)}, f32[768]{0:T(1024)}, u32[]{:S(2)}) copy-start(f32[768]{0:T(1024)} %param.41) | copy-start | bytes 9220
  1510.3 135.6 %copy-start.27 = (f32[64,1024]{1,0:T(8,128)S(1)}, f32[64,1024]{1,0:T(8,128)}, u32[]{:S(2)}) copy-start(f32[64,1024]{1,0:T(8,128)} %param.28) | copy-start | bytes 786436
  1510.3 135.6 %copy-start.35 = (f32[64,1024]{1,0:T(8,128)S(1)}, f32[64,1024]{1,0:T(8,128)}, u32[]{:S(2)}) copy-start(f32[64,1024]{1,0:T(8,128)} %param.33) | copy-start | bytes 786436
  1510.3 137.6 %copy-start.18 = (f32[64,3072]{1,0:T(8,128)S(1)}, f32[64,3072]{1,0:T(8,128)}, u32[]{:S(2)}) copy-start(f32[64,3072]{1,0:T(8,128)} %param.27) | copy-start | bytes 2359300
  (63 other events, 833.8 us)
Sparse Core Ops, SparseCore 0:
  11.4 97.0 all-gather.5
  111.8 59.0 all-gather.7
  174.2 111.4 all-gather.9
  288.9 111.0 all-gather.11
  462.6 93.2 reduce-scatter.6
  596.5 202.2 reduce-scatter.4
  801.1 345.9 reduce-scatter.10
  1149.6 351.9 reduce-scatter.8
  1505.5 26.1 all-reduce.6
where the time goes:
time: 1670 us; the launch traced here: 1660 us
  waiting for transfers between devices  1050 us (63%)
  matrix products  207 us (12%)
  blocking collectives  162 us (10%)
  local copies, waits for them, and re-layouts  111 us (7%)
  other arithmetic  108 us (6%)
  between operations  21 us (1%)
    reduce_scatter x1, waiting for transfers between devices, shards(): lax.psum_scatter(terms[2], 'fsdp', scatter_dimension=0, tiled=True)  352 us
    reduce_scatter x1, waiting for transfers between devices, shards(): lax.psum_scatter(terms[3], 'fsdp', scatter_dimension=0, tiled=True)  347 us
    reduce_scatter x1, waiting for transfers between devices, shards(): lax.psum_scatter(terms[0], 'fsdp', scatter_dimension=0, tiled=True)  110 us
    all_gather x1, waiting for transfers between devices, shards(): lax.all_gather(up_weight.astype(half), 'fsdp', axis=0, tiled=True)  104 us
    all_gather x1, waiting for transfers between devices, shards(): lax.all_gather(down_weight.astype(half), 'fsdp', axis=0, tiled=True)  97.1 us
    unnamed x1, blocking collectives  79.4 us
    all_gather x1, blocking collectives, shards(): lax.all_gather(small_params.astype(half), 'fsdp', axis=0, tiled=True)  43.1 us
    all_gather x1, waiting for transfers between devices, shards(): lax.all_gather(qkv_weight.astype(half), 'fsdp', axis=0, tiled=True)  41.3 us
  transfers between devices with their start and end apart: 9, of which 6 were waited for; matrix products, arithmetic and copies ran while one was open for 20% of the time, Pallas kernels for 0%

commit v1 on v0

v1 whole, which is shorter than its diff:
```python
import math

import jax
import jax.numpy as jnp
from jax import lax
from jax.experimental import pallas as pl
from jax.experimental.pallas import tpu as pltpu
from jax.sharding import PartitionSpec as P

HD = 64
STEP = 10
EPS_NORM = 1e-06
CLIP = 1.0
RATE = 0.04
RATE_SMALL = 0.25
DECAY = 0.05
BETA_ONE = 0.9
BETA_TWO = 0.999
EPS_ADAM = 1e-08
F32 = jnp.float32
BF = jnp.bfloat16
BOTH = ("grp", "fsdp")
SWAP = [(0, 1), (1, 0)]
ANY = pl.BlockSpec(memory_space=pl.ANY)
SMEM = pl.BlockSpec(memory_space=pltpu.SMEM)
TILE = 128
SPAN = 256


def dims(n):
    m = max(1, math.isqrt(n // 4))
    return n // (m * m), m


def build_perms(n):
    nz, m = dims(n)

    def chip(z, y, x):
        return (z % nz) * m * m + (y % m) * m + x % m

    def build(move):
        return [
            (c * n + chip(z, y, x), c * n + chip(*move(c, z, y, x)))
            for c in range(2)
            for z in range(nz)
            for y in range(m)
            for x in range(m)
        ]

    return {
        "z": [build(lambda c, z, y, x: (z + k, y, x)) for k in range(nz)],
        "a": [build(lambda c, z, y, x: (z, y, x + k) if c == 0 else (z, y + k, x)) for k in range(m)],
        "b": [build(lambda c, z, y, x: (z, y + k, x) if c == 0 else (z, y, x + k)) for k in range(m)],
        "x": [build(lambda c, z, y, x: (z, y, x + k)) for k in range(m)],
        "y": [build(lambda c, z, y, x: (z, y + k, x)) for k in range(m)],
    }


def send(value, table):
    return lax.ppermute(value, BOTH, table)


def layer_norm(x, gain, bias):
    mean = jnp.mean(x, -1, keepdims=True)
    centred = x - mean
    var = jnp.mean(centred * centred, -1, keepdims=True)
    return centred * lax.rsqrt(var + EPS_NORM) * gain + bias


def unpack(small, width, hidden):
    pieces = [small[i * width : (i + 1) * width] for i in range(7)]
    return pieces + [small[7 * width : 7 * width + hidden], small[7 * width + hidden :]]


def adam(weight, first, second, grad, decay, rate):
    first = BETA_ONE * first + (1.0 - BETA_ONE) * grad
    second = BETA_TWO * second + (1.0 - BETA_TWO) * grad * grad
    step_size = (
        first / (1.0 - BETA_ONE**STEP) / (jnp.sqrt(second / (1.0 - BETA_TWO**STEP)) + EPS_ADAM)
    )
    return (weight - rate * (step_size + decay * weight), first, second)


def after(value, *deps):
    return lax.optimization_barrier((value, *deps))[0]


def gather_pieces(own, perms, nz, m):
    first = jnp.stack([own] + [send(own, perms["z"][k]) for k in range(1, nz)])
    second = [first] + [send(first, perms["a"][k]) for k in range(1, m)]
    mine = []
    for piece in second:
        mine += [piece] + [send(piece, perms["b"][k]) for k in range(1, m)]
    return mine, [lax.ppermute(p, "grp", SWAP) for p in mine]


def assemble(coords, mine, other, nz, m, shapes, plan, name):
    def kernel(*refs):
        coord = refs[0]
        sources = refs[1 : 1 + 2 * m * m]
        outs = refs[1 + 2 * m * m : 1 + 2 * m * m + len(shapes)]
        sem = refs[-1]
        z, y, x, c = coord[0], coord[1], coord[2], coord[3]
        for side in range(2):
            core = c if side == 0 else 1 - c
            for ia in range(m):
                for ib in range(m):
                    src = sources[side * m * m + ia * m + ib]
                    dx = jnp.where(core == 0, ia, ib)
                    dy = jnp.where(core == 0, ib, ia)
                    px = lax.rem(x - dx + m, m)
                    py = lax.rem(y - dy + m, m)
                    for dz in range(nz):
                        pz = lax.rem(z - dz + nz, nz)
                        chip = (pz * m + py) * m + px
                        for out, row, rows, col, cols, scol in plan(chip, core):
                            pltpu.make_async_copy(
                                src.at[dz, :, pl.ds(scol, cols)],
                                outs[out].at[
                                    pl.ds(pl.multiple_of(row, 16), rows),
                                    pl.ds(pl.multiple_of(col, 128), cols),
                                ],
                                sem.at[out],
                            ).start()
        for i, ref in enumerate(outs):
            pltpu.make_async_copy(ref, ref, sem.at[i]).wait()

    total = sum(2 * math.prod(s) for s in shapes)
    return pl.pallas_call(
        kernel,
        out_shape=[jax.ShapeDtypeStruct(s, BF) for s in shapes],
        in_specs=[SMEM] + [ANY] * (2 * m * m),
        out_specs=[pl.BlockSpec(memory_space=pltpu.VMEM)] * len(shapes),
        scratch_shapes=[pltpu.SemaphoreType.DMA((len(shapes),))],
        compiler_params=pltpu.CompilerParams(vmem_limit_bytes=24 << 20),
        cost_estimate=pl.CostEstimate(flops=0, bytes_accessed=2 * total, transcendentals=0),
        name=name,
    )(coords, *mine, *other)


def weight_grad(coords, scale, left, right, side, nz, m, name):
    tokens, total = left.shape
    half = right.shape[1] // 2
    n = nz * m * m
    r = total // n
    zrows = total // nz
    mt = min(256, zrows)
    nt = min(512, half)
    mc, nc = zrows // mt, half // nt

    def kernel(coord, scale_ref, x_hbm, y_hbm, *refs):
        outs = refs[:m]
        xv, yv, acc, xsem, ysem, osem = refs[m:]
        z, y, x, c = coord[0], coord[1], coord[2], coord[3]
        owner = c if side == 0 else 1 - c
        weight = scale_ref[0]

        def xcopy(dz, i):
            pz = lax.rem(z + dz, nz)
            return pltpu.make_async_copy(
                x_hbm.at[:, pl.ds(pl.multiple_of(pz * zrows + i * mt, 128), mt)],
                xv.at[dz * mc + i],
                xsem.at[dz * mc + i],
            )

        def ycopy(j):
            return pltpu.make_async_copy(
                y_hbm.at[:, pl.ds(pl.multiple_of(owner * half + j * nt, 128), nt)],
                yv.at[j],
                ysem.at[j],
            )

        xcopy(0, 0).start()
        for j in range(nc):
            ycopy(j).start()
        for dz in range(nz):
            for i in range(mc):
                if dz or i:
                    xcopy(dz, i).start()
        copies = []
        for dz in range(nz):
            for i in range(mc):
                xcopy(dz, i).wait()
                if dz == 0 and i == 0:
                    for j in range(nc):
                        ycopy(j).wait()

                def step(j, carry):
                    out = lax.dot_general(
                        xv[dz * mc + i],
                        yv[j],
                        (((0,), (0,)), ((), ())),
                        preferred_element_type=F32,
                    )
                    acc[dz, i * mt : (i + 1) * mt, pl.ds(pl.multiple_of(j * nt, 128), nt)] = (
                        out * weight
                    ).astype(BF)
                    return carry

                lax.fori_loop(0, nc, step, 0)
            for ib in range(m):
                for ia in range(m):
                    dx = jnp.where(owner == 0, ia, ib)
                    dy = jnp.where(owner == 0, ib, ia)
                    px = lax.rem(x + dx, m)
                    py = lax.rem(y + dy, m)
                    copy = pltpu.make_async_copy(
                        acc.at[dz, pl.ds(pl.multiple_of((py * m + px) * r, 16), r), :],
                        outs[ib].at[ia, dz],
                        osem.at[dz, ib * m + ia],
                    )
                    copy.start()
                    copies.append(copy)
        for copy in copies:
            copy.wait()

    return pl.pallas_call(
        kernel,
        out_shape=[jax.ShapeDtypeStruct((m, nz, r, half), BF)] * m,
        in_specs=[SMEM, SMEM, ANY, ANY],
        out_specs=[ANY] * m,
        scratch_shapes=[
            pltpu.VMEM((nz * mc, tokens, mt), BF),
            pltpu.VMEM((nc, tokens, nt), BF),
            pltpu.VMEM((nz, zrows, half), BF),
            pltpu.SemaphoreType.DMA((nz * mc,)),
            pltpu.SemaphoreType.DMA((nc,)),
            pltpu.SemaphoreType.DMA((nz, m * m)),
        ],
        compiler_params=pltpu.CompilerParams(vmem_limit_bytes=40 << 20),
        cost_estimate=pl.CostEstimate(
            flops=2 * tokens * total * half,
            bytes_accessed=2 * (tokens * total + tokens * half + total * half),
            transcendentals=0,
        ),
        name=name,
    )(coords, scale, left, right)


def reduce_pieces(mine, other, perms, nz, m):
    got = [lax.ppermute(p, "grp", SWAP) for p in other]
    sums = [None] * m
    for k in list(range(1, m)) + [0]:
        sums[k] = (mine[k].astype(F32) + got[k].astype(F32)).astype(BF)
    for axis, size, nxt in (("b", m, m), ("a", m, nz), ("z", nz, 0)):
        recv = [send(sums[k], perms[axis][k]) for k in range(1, size)]

        def total(pick):
            t = pick(sums[0]).astype(F32)
            for other_part in recv:
                t = t + pick(other_part).astype(F32)
            return t

        if not nxt:
            return total(lambda v: v)
        sums = [total(lambda v, k=k: v[k]).astype(BF) for k in range(nxt)]


def head_stack(block, low_lanes):
    zero = jnp.zeros_like(block)
    return jnp.concatenate(
        [jnp.where(low_lanes, block, zero), jnp.where(low_lanes, zero, block)], 0
    )


def tile_start(t, rows):
    return pl.multiple_of(jnp.clip(t * TILE - (SPAN - TILE) // 2, 0, rows - SPAN), 64)


def tile_mask(seg_col, seg_row, t, start):
    same = seg_col[pl.ds(start, SPAN), :] == seg_row[:, pl.ds(pl.multiple_of(t * TILE, 128), TILE)]
    return jnp.concatenate([same, same], 1)


def probabilities(keys, stack, same):
    scores = lax.dot_general(keys, stack, (((1,), (1,)), ((), ())), preferred_element_type=F32)
    scores = jnp.where(same, scores * HD**-0.5, -1e30)
    expo = jnp.exp(scores - jnp.max(scores, 0, keepdims=True))
    return expo * (1.0 / jnp.sum(expo, 0, keepdims=True))


def attention(project, seg_col, seg_row):
    rows, width = project.shape[0], project.shape[1] // 3
    pairs = width // (2 * HD)

    def kernel(col_ref, row_ref, q_ref, k_ref, v_ref, out_ref):
        t = pl.program_id(0)
        start = tile_start(t, rows)
        same = tile_mask(col_ref, row_ref, t, start)
        low = lax.broadcasted_iota(jnp.int32, (TILE, 2 * HD), 1) < HD
        for h in range(pairs):
            lanes = slice(h * 2 * HD, (h + 1) * 2 * HD)
            probs = probabilities(k_ref[pl.ds(start, SPAN), lanes], head_stack(q_ref[:, lanes], low), same)
            mixed = lax.dot_general(
                probs.astype(BF),
                v_ref[pl.ds(start, SPAN), lanes],
                (((0,), (0,)), ((), ())),
                preferred_element_type=F32,
            )
            out_ref[:, lanes] = jnp.where(low, mixed[:TILE], mixed[TILE:]).astype(BF)

    return pl.pallas_call(
        kernel,
        grid=(rows // TILE,),
        out_shape=jax.ShapeDtypeStruct((rows, width), BF),
        in_specs=[
            pl.BlockSpec((rows, 1), lambda t: (0, 0)),
            pl.BlockSpec((1, rows), lambda t: (0, 0)),
            pl.BlockSpec((TILE, width), lambda t: (t, 0)),
            pl.BlockSpec((rows, width), lambda t: (0, 1)),
            pl.BlockSpec((rows, width), lambda t: (0, 2)),
        ],
        out_specs=pl.BlockSpec((TILE, width), lambda t: (t, 0)),
        compiler_params=pltpu.CompilerParams(vmem_limit_bytes=32 << 20),
        cost_estimate=pl.CostEstimate(
            flops=8 * 10**9, bytes_accessed=8 * rows * width, transcendentals=rows * SPAN * 2 * pairs
        ),
        name="attention",
    )(seg_col, seg_row, project, project, project)


def attention_back(project, grad, seg_col, seg_row):
    rows, width = project.shape[0], project.shape[1] // 3
    pairs = width // (2 * HD)
    tiles = rows // TILE

    def kernel(col_ref, row_ref, q_ref, k_ref, v_ref, g_ref, out_ref, dk, dv):
        t = pl.program_id(0)

        @pl.when(t == 0)
        def _():
            dk[...] = jnp.zeros_like(dk)
            dv[...] = jnp.zeros_like(dv)

        start = tile_start(t, rows)
        window = pl.ds(start, SPAN)
        same = tile_mask(col_ref, row_ref, t, start)
        low = lax.broadcasted_iota(jnp.int32, (TILE, 2 * HD), 1) < HD
        scale = HD**-0.5
        for h in range(pairs):
            lanes = slice(h * 2 * HD, (h + 1) * 2 * HD)
            keys, values = k_ref[window, lanes], v_ref[window, lanes]
            queries = head_stack(q_ref[:, lanes], low)
            grads = head_stack(g_ref[:, lanes], low)
            probs = probabilities(keys, queries, same)
            grad_probs = lax.dot_general(
                values, grads, (((1,), (1,)), ((), ())), preferred_element_type=F32
            )
            inner = jnp.sum(probs * grad_probs, 0, keepdims=True)
            grad_scores = (probs * (grad_probs - inner)).astype(BF)
            dv[window, lanes] += jnp.dot(probs.astype(BF), grads, preferred_element_type=F32)
            dk[window, lanes] += jnp.dot(grad_scores, queries, preferred_element_type=F32)
            dq = lax.dot_general(
                grad_scores, keys, (((0,), (0,)), ((), ())), preferred_element_type=F32
            )
            out_ref[pl.ds(pl.multiple_of(t * TILE, TILE), TILE), lanes] = (
                jnp.where(low, dq[:TILE], dq[TILE:]) * scale
            ).astype(BF)

        @pl.when(t == tiles - 1)
        def _():
            out_ref[:, width : 2 * width] = (dk[...] * scale).astype(BF)
            out_ref[:, 2 * width :] = dv[...].astype(BF)

    return pl.pallas_call(
        kernel,
        grid=(tiles,),
        out_shape=jax.ShapeDtypeStruct((rows, 3 * width), BF),
        in_specs=[
            pl.BlockSpec((rows, 1), lambda t: (0, 0)),
            pl.BlockSpec((1, rows), lambda t: (0, 0)),
            pl.BlockSpec((TILE, width), lambda t: (t, 0)),
            pl.BlockSpec((rows, width), lambda t: (0, 1)),
            pl.BlockSpec((rows, width), lambda t: (0, 2)),
            pl.BlockSpec((TILE, width), lambda t: (t, 0)),
        ],
        out_specs=pl.BlockSpec((rows, 3 * width), lambda t: (0, 0)),
        scratch_shapes=[pltpu.VMEM((rows, width), F32), pltpu.VMEM((rows, width), F32)],
        compiler_params=pltpu.CompilerParams(vmem_limit_bytes=48 << 20),
        cost_estimate=pl.CostEstimate(
            flops=16 * 10**9, bytes_accessed=14 * rows * width, transcendentals=rows * SPAN * 2 * pairs
        ),
        name="attention_back",
    )(seg_col, seg_row, project, project, project, grad)


def shards(
    tokens, cotangent, segment_ids, group_counts,
    qkv_weight, out_weight, up_weight, down_weight, small_params,
    qkv_first, out_first, up_first, down_first, small_first,
    qkv_second, out_second, up_second, down_second, small_second,
):
    width = tokens.shape[1]
    hidden = up_weight.shape[1]
    rows = tokens.shape[0]
    n = lax.axis_size("fsdp")
    nz, m = dims(n)
    perms = build_perms(n)
    chip = lax.axis_index("fsdp")
    core = lax.axis_index("grp")
    z, y, x = chip // (m * m), chip // m % m, chip % m
    coords = jnp.stack([z, y, x, core]).astype(jnp.int32)
    r = qkv_weight.shape[0]
    ratio = down_weight.shape[0] // r

    counts = group_counts.astype(F32)
    share = counts / jnp.sum(counts)
    is_local = core >= lax.axis_size("grp") // 2
    mine = jnp.where(is_local, share[1], share[0])
    scale = mine.reshape(1)

    def half(w):
        cols = w.shape[1] // 2
        return lax.dynamic_slice_in_dim(w, core * cols, cols, 1).astype(BF)

    piece = small_params.astype(BF)
    stack = jnp.stack([piece] + [send(piece, perms["z"][k]) for k in range(1, nz)])
    stack = jnp.stack([stack] + [send(stack, perms["y"][k]) for k in range(1, m)])
    stack = jnp.stack([stack] + [send(stack, perms["x"][k]) for k in range(1, m)])
    index = jnp.arange(n)
    place = (((x - index % m) % m) * m + (y - index // m % m) % m) * nz + (z - index // (m * m)) % nz
    small_full = jnp.take(stack.reshape(n, -1), place, axis=0).reshape(-1).astype(F32)
    gain_one, bias_one, bias_query, bias_value, bias_out, gain_two, bias_two, bias_up, bias_down = (
        unpack(small_full, width, hidden)
    )

    own_one = jnp.concatenate([half(qkv_weight), half(out_weight)], 1)
    own_two = half(up_weight)
    low_down = half(down_weight)
    own_three = jnp.concatenate([low_down[s * r : (s + 1) * r] for s in range(ratio)], 1)
    hq, ho, hu = 3 * width // 2, width // 2, hidden // 2

    mine_one, other_one = gather_pieces(own_one, perms, nz, m)
    qkv_full, out_full = assemble(
        coords, mine_one, other_one, nz, m, [(width, 3 * width), (width, width)],
        lambda chip, c: [(0, chip * r, r, c * hq, hq, 0), (1, chip * r, r, c * ho, ho, hq)],
        "assemble_qkv_out",
    )
    mine_two, other_two = gather_pieces(own_two, perms, nz, m)
    (up_full,) = assemble(
        coords, mine_two, other_two, nz, m, [(width, hidden)],
        lambda chip, c: [(0, chip * r, r, c * hu, hu, 0)],
        "assemble_up",
    )
    mine_three, other_three = gather_pieces(own_three, perms, nz, m)
    (down_full,) = assemble(
        coords, mine_three, other_three, nz, m, [(hidden, width)],
        lambda chip, c: [
            (0, (chip * ratio + s) * r, r, c * ho, ho, s * ho) for s in range(ratio)
        ],
        "assemble_down",
    )

    inputs = tokens.astype(F32)
    normed_one = layer_norm(inputs, gain_one, bias_one).astype(BF)
    qkv_bias = jnp.concatenate([bias_query, jnp.zeros_like(bias_query), bias_value])
    project = (jnp.dot(normed_one, qkv_full, preferred_element_type=F32) + qkv_bias).astype(BF)
    seg_col, seg_row = segment_ids.reshape(rows, 1), segment_ids.reshape(1, rows)
    att = attention(project, seg_col, seg_row)
    middle = inputs + jnp.dot(att, out_full, preferred_element_type=F32) + bias_out
    normed_two = layer_norm(middle, gain_two, bias_two).astype(BF)
    pre_act = jnp.dot(normed_two, up_full, preferred_element_type=F32) + bias_up
    act = jax.nn.gelu(pre_act).astype(BF)
    output = middle + jnp.dot(act, down_full, preferred_element_type=F32) + bias_down
    block_output = output.astype(BF)

    def reduced(left, right, name):
        other = weight_grad(coords, scale, left, right, 1, nz, m, name + "_other")
        own = weight_grad(coords, scale, left, right, 0, nz, m, name + "_own")
        return reduce_pieces(own, other, perms, nz, m), own[0]

    grad_out = cotangent.astype(F32)
    grad_bias_down = jnp.sum(grad_out, 0)
    half_down, done = reduced(act, cotangent, "grad_down")
    grad_act = jnp.einsum("td,fd->tf", after(cotangent, done), down_full, preferred_element_type=F32)
    grad_pre = jax.vjp(jax.nn.gelu, pre_act)[1](grad_act)[0].astype(BF)
    grad_bias_up = jnp.sum(grad_pre.astype(F32), 0)
    half_up, done = reduced(normed_two, grad_pre, "grad_up")
    grad_normed_two = jnp.einsum("tf,df->td", after(grad_pre, done), up_full, preferred_element_type=F32)
    grad_mid, grad_gain_two, grad_bias_two = jax.vjp(layer_norm, middle, gain_two, bias_two)[1](
        grad_normed_two
    )
    grad_mid = grad_out + grad_mid
    grad_mid_low = grad_mid.astype(BF)
    grad_bias_out = jnp.sum(grad_mid_low.astype(F32), 0)
    half_out, done = reduced(att, grad_mid_low, "grad_out")
    grad_att = jnp.einsum("te,de->td", after(grad_mid_low, done), out_full, preferred_element_type=F32).astype(BF)
    grad_project = attention_back(project, grad_att, seg_col, seg_row)
    half_qkv, done = reduced(normed_one, grad_project, "grad_qkv")
    grad_project = after(grad_project, done)
    grad_project_wide = grad_project.astype(F32)
    grad_bias_query = jnp.sum(grad_project_wide[:, :width], 0)
    grad_bias_value = jnp.sum(grad_project_wide[:, 2 * width :], 0)
    grad_normed_one = jnp.einsum("te,de->td", grad_project, qkv_full, preferred_element_type=F32)
    grad_in, grad_gain_one, grad_bias_one = jax.vjp(layer_norm, inputs, gain_one, bias_one)[1](
        grad_normed_one
    )
    tokens_grad = (grad_mid + grad_in).astype(BF)

    grad_small = mine * jnp.concatenate(
        [
            grad_gain_one, grad_bias_one, grad_bias_query, grad_bias_value, grad_bias_out,
            grad_gain_two, grad_bias_two, grad_bias_up, grad_bias_down,
        ]
    )
    part = (grad_small + lax.ppermute(grad_small, "grp", SWAP)).reshape(nz, m, m, -1)
    for axis, at, size, dim in (("y", y, m, 1), ("x", x, m, 1), ("z", z, nz, 0)):
        recv = [
            send(lax.dynamic_index_in_dim(part, (at + k) % size, dim, False), perms[axis][k])
            for k in range(1, size)
        ]
        part = lax.dynamic_index_in_dim(part, at, dim, False)
        for piece in recv:
            part = part + piece
    merged_small = part

    def joined(piece):
        low = piece.astype(BF)
        got = lax.ppermute(low, "grp", SWAP)
        left = jnp.where(core == 0, low, got)
        right = jnp.where(core == 0, got, low)
        return jnp.concatenate([left, right], 1).astype(F32)

    merged = tuple(joined(p) for p in (half_qkv, half_out, half_up, half_down)) + (merged_small,)
    total_sq = sum((jnp.sum(piece * piece) for piece in merged)).reshape(1, 1)
    for axis, size in (("x", m), ("y", m), ("z", nz)):
        got = [total_sq] + [send(total_sq, perms[axis][k]) for k in range(1, size)]
        while len(got) > 1:
            step = len(got) // 2
            got = [got[k] + got[k + step] for k in range(step)]
        total_sq = got[0]
    total_sq = total_sq[0, 0]
    clip = jnp.minimum(1.0, CLIP * lax.rsqrt(total_sq))
    olds = (qkv_weight, out_weight, up_weight, down_weight, small_params)
    firsts = (qkv_first, out_first, up_first, down_first, small_first)
    seconds = (qkv_second, out_second, up_second, down_second, small_second)
    decays = (DECAY, DECAY, DECAY, DECAY, 0.0)
    rates = (RATE, RATE, RATE, RATE, RATE_SMALL)
    results = [
        adam(w, f, s, g * clip, dc, rt)
        for w, f, s, g, dc, rt in zip(olds, firsts, seconds, merged, decays, rates)
    ]
    return (
        block_output,
        tokens_grad,
        *[res[0] for res in results],
        *[res[1] for res in results],
        *[res[2] for res in results],
        total_sq,
    )


def solution(mesh):
    token, flat, row, vec = P(BOTH, None), P(BOTH), P("fsdp", None), P("fsdp")
    params = (row, row, row, row, vec)
    return jax.shard_map(
        shards,
        mesh=mesh,
        in_specs=(token, token, flat, P()) + params * 3,
        out_specs=(token, token) + params * 3 + (P(),),
        check_vma=False,
    )
```

time: 1670 us -> 627 us (0.38)
  waiting for transfers between devices: 1050 us -> 163 us
  blocking collectives: 162 us -> 0 us
  Pallas kernels: 0 us -> 128 us
  starting transfers between devices: 0.37 us -> 124 us
  matrix products: 207 us -> 97.3 us
  local copies, waits for them, and re-layouts: 111 us -> 36.5 us
  other arithmetic: 108 us -> 64.1 us
    reduce_scatter x4 -> x0, waiting for transfers between devices: 809 us -> none  [the longest x1 352 us: shards(): lax.psum_scatter(terms[2], 'fsdp', scatter_dimension=0, tiled=True)]
    all_gather x4 -> x0, waiting for transfers between devices: 242 us -> none  [the longest x1 104 us: shards(): lax.all_gather(up_weight.astype(half), 'fsdp', axis=0, tiled=True)]
    ppermute x0 -> x78, waiting for transfers between devices: none -> 163 us  [the longest x53 160 us: send(): return lax.ppermute(value, BOTH, table)]
    pallas_call x0 -> x13, Pallas kernels: none -> 128 us  [the longest x8 72 us: weight_grad(): pl.pallas_call(kernel, out_shape=[jax.ShapeDtypeStruct((m, nz, r, half),...]
    ppermute x0 -> x78, starting transfers between devices: none -> 124 us  [the longest x53 105 us: send(): return lax.ppermute(value, BOTH, table)]
    dot_general x26 -> x8, matrix products: 207 us -> 97.3 us  [the longest x1 25.7 us: shards(): jnp.einsum('td,fd->tf', after(cotangent, done), down_full, preferred_elem...]
    unnamed x1 -> x0, blocking collectives: 79.4 us -> none
    all_gather x1 -> x0, blocking collectives: 43.1 us -> none  [shards(): lax.all_gather(small_params.astype(half), 'fsdp', axis=0, tiled=True)]
  transfers between devices with their start and end apart: 9 -> 78, of which waited for: 6 -> 24; matrix products, arithmetic and copies ran while one was open for 20% -> 14% of each run, Pallas kernels for 0% -> 10%
where the time goes in v1:
time: 627 us; the launch traced here: 623 us
  waiting for transfers between devices  163 us (26%)
  Pallas kernels  128 us (20%)
  starting transfers between devices  124 us (20%)
  matrix products  97.3 us (16%)
  other arithmetic  64.1 us (10%)
  local copies, waits for them, and re-layouts  36.5 us (6%)
  between operations  11.2 us (2%)
    ppermute x53, waiting for transfers between devices, send(): return lax.ppermute(value, BOTH, table)  160 us
    ppermute x53, starting transfers between devices, send(): return lax.ppermute(value, BOTH, table)  105 us
    pallas_call x8, Pallas kernels, weight_grad(): pl.pallas_call(kernel, out_shape=[jax.ShapeDtypeStruct((m, nz, r, half),...  72 us
    pallas_call x1, Pallas kernels, attention_back(): pl.pallas_call(kernel, grid=(tiles,), out_shape=jax.ShapeDtypeStruct((row...  33.3 us
    unnamed x156, local copies, waits for them, and re-layouts  27.6 us
    dot_general x1, matrix products, shards(): jnp.einsum('td,fd->tf', after(cotangent, done), down_full, preferred_elem...  25.7 us
    dot_general x1, matrix products, shards(): pre_act = jnp.dot(normed_two, up_full, preferred_element_type=F32) + bias_up  20.7 us
    ppermute x12, starting transfers between devices, gather_pieces(): return (mine, [lax.ppermute(p, 'grp', SWAP) for p in mine])  16 us
  transfers between devices with their start and end apart: 78, of which 24 were waited for; matrix products, arithmetic and copies ran while one was open for 14% of the time, Pallas kernels for 10%

profile of v1, /device:TPU:0, one launch (start us, length us, event | category | flops | bytes accessed | tf_op | source)
XLA Modules:
  0.0 623.2 jit_solution(5635169180408963574)
XLA Ops:
  65.2 9.6 %collective-permute-start.26 = (bf16[64,2048]{1,0:T(8,128)(2,1)}, bf16[64,2048]{1,0:T(8,128)(2,1)}, u32[]{:S(2)}, u32[]{:S(2)}) collective-permute-start(bf16[64,2048]{1,0:T(8,128)(2,1)} %get-tuple-element.127), channel_id=1, source_target_pairs={{0,8},{1,9},{2,10},{3,11},{4,12},{5,13},{6,14},{7,15},{8,0},{9,1},... | collective-permute-start | bytes 786440 | tf_op jit(solution)/shard_map/ppermute | solution.py:60
  86.5 12.7 %collective-permute-start.11 = (bf16[4,64,2048]{2,1,0:T(8,128)(2,1)S(1)}, bf16[4,64,2048]{2,1,0:T(8,128)(2,1)}, u32[]{:S(2)}, u32[]{:S(2)}) collective-permute-start(bf16[4,64,2048]{2,1,0:T(8,128)(2,1)S(1)} %pad_maximum_fusion.refs_1_), channel_id=1, source_target_pairs={{0,16},{16,0},{1,17},{17,1},{2,18},{18,2},{3,19},{19,3},{4,20},{20... | collective-permute-start | bytes 3145736 | tf_op jit(solution)/shard_map/ppermute | solution.py:94
  121.9 7.1 %add_convert_fusion.q_ref.k_ref.v_ref = bf16[1024,3072]{1,0:T(8,128)(2,1)S(1)} fusion(f32[3072]{0:T(1024)S(1)} %pad_maximum_fusion.11, bf16[1024,1024]{1,0:T(8,128)(2,1)S(1)} %fusion.14.x_hbm, bf16[1024,3072]{1,0:T(8,128)(2,1)S(1)} %get-tuple-element.40), kind=kOutput, calls=%fused_computation.12 | convolution fusion | flops 6448742400 | bytes 14692352 | tf_op jit(solution)/shard_map/dot_general | solution.py:457
  129.1 12.6 %attention.1.x_hbm = bf16[1024,1024]{1,0:T(8,128)(2,1)S(1)} custom-call(s32[1024,1]{1,0:T(8,128)S(1)} %copy-done.23, s32[1,1024]{1,0:T(1,128)S(1)} %bitcast.196, bf16[1024,3072]{1,0:T(8,128)(2,1)S(1)} %add_convert_fusion.q_ref.k_ref.v_ref, bf16[1024,3072]{1,0:T(8,128)(2,1)S(1)} %add_convert_fusion.q_ref.k_ref.v_ref, ...), custom_call_target="tpu_custom_call" | custom-call | flops 8000000000 | bytes 8388608 | tf_op jit(solution)/shard_map/attention/pallas_call | solution.py:302
  146.4 16.2 %collective-permute-done.20.refs_4_ = bf16[4,64,2048]{2,1,0:T(8,128)(2,1)S(1)} collective-permute-done((bf16[4,64,2048]{2,1,0:T(8,128)(2,1)}, bf16[4,64,2048]{2,1,0:T(8,128)(2,1)S(1)}, u32[]{:S(2)}, u32[]{:S(2)}) %collective-permute-start.20) | collective-permute-done | bytes 1048608 | tf_op jit(solution)/shard_map/ppermute | solution.py:60
  166.3 7.6 %collective-permute-done.30.refs_4_ = bf16[4,64,2048]{2,1,0:T(8,128)(2,1)S(1)} collective-permute-done((bf16[4,64,2048]{2,1,0:T(8,128)(2,1)}, bf16[4,64,2048]{2,1,0:T(8,128)(2,1)S(1)}, u32[]{:S(2)}, u32[]{:S(2)}) %collective-permute-start.30) | collective-permute-done | bytes 1048608 | tf_op jit(solution)/shard_map/ppermute | solution.py:60
  175.8 20.7 %multiply_convert_fusion = (bf16[1024,4096]{1,0:T(8,128)(2,1)}, f32[1024,4096]{1,0:T(8,128)}) fusion(f32[4096]{0:T(1024)S(1)} %slice.285, bf16[1024,1024]{1,0:T(8,128)(2,1)} %add_convert_fusion.7.x_hbm, bf16[1024,4096]{1,0:T(8,128)(2,1)S(1)} %assemble_up.1), kind=kOutput, calls=%fused_computation.11 | convolution fusion | flops 8631877632 | bytes 35667968 | tf_op jit(solution)/shard_map/dot_general | solution.py:462
  196.6 9.7 %grad_down_own.1 = (bf16[2,4,256,512]{3,2,1,0:T(8,128)(2,1)S(1)}, bf16[2,4,256,512]{3,2,1,0:T(8,128)(2,1)S(1)}) custom-call(s32[4]{0:T(128)S(1)} %pad_add_fusion.refs_0_.coord, f32[1]{0:T(128)} %bitcast.25.scale_ref, bf16[1024,4096]{1,0:T(8,128)(2,1)} %get-tuple-element.152.x_hbm, bf16[1024,1024]{1,0:T(8,128)(2,1)S(1)} %copy-done.2), custom_call_target="tpu_custom_call" | custom-call | flops 4294967296 | bytes 13631488 | tf_op jit(solution)/shard_map/grad_down_own/pallas_call | solution.py:217
  208.9 9.9 %grad_down_other.1 = (bf16[2,4,256,512]{3,2,1,0:T(8,128)(2,1)S(1)}, bf16[2,4,256,512]{3,2,1,0:T(8,128)(2,1)S(1)}) custom-call(s32[4]{0:T(128)S(1)} %pad_add_fusion.refs_0_.coord, f32[1]{0:T(128)} %bitcast.25.scale_ref, bf16[1024,4096]{1,0:T(8,128)(2,1)} %get-tuple-element.152.x_hbm, bf16[1024,1024]{1,0:T(8,128)(2,1)S(1)} %copy-done.2), custom_call_target="tpu_custom_call" | custom-call | flops 4294967296 | bytes 13631488 | tf_op jit(solution)/shard_map/grad_down_other/pallas_call | solution.py:217
  226.4 25.7 %convert_reduce_fusion = (f32[4096]{0:T(1024)S(1)}, bf16[1024,4096]{1,0:T(8,128)(2,1)}) fusion(f32[1024,4096]{1,0:T(8,128)} %get-tuple-element.153, f32[4096]{0:T(1024)S(1)} %slice.285, bf16[1024,1024]{1,0:T(8,128)(2,1)} %y_hbm.3, bf16[4096,1024]{1,0:T(8,128)(2,1)} %copy-done), kind=kOutput, calls=%fused_computation.10 | convolution fusion | flops 8686399488 | bytes 35684352 | tf_op jit(solution)/shard_map/td,fd->tf/dot_general | solution.py:475
  253.7 11.1 %grad_up_own.1 = (bf16[2,4,64,2048]{3,2,1,0:T(8,128)(2,1)S(1)}, bf16[2,4,64,2048]{3,2,1,0:T(8,128)(2,1)S(1)}) custom-call(s32[4]{0:T(128)S(1)} %pad_add_fusion.refs_0_.coord, f32[1]{0:T(128)} %bitcast.25.scale_ref, bf16[1024,1024]{1,0:T(8,128)(2,1)S(1)} %copy-done.14, bf16[1024,4096]{1,0:T(8,128)(2,1)} %get-tuple-element.45.y_hbm), custom_call_target="tpu_custom_call" | custom-call | flops 4294967296 | bytes 10485760 | tf_op jit(solution)/shard_map/grad_up_own/pallas_call | solution.py:217
  267.5 14.7 %multiply_reduce_fusion = (f32[1024]{0:T(1024)S(1)}, f32[1024]{0:T(1024)S(1)}, f32[1024]{0:T(1024)S(1)}, f32[1024,1024]{1,0:T(8,128)S(1)}) fusion(f32[1024,1024]{1,0:T(8,128)S(1)} %copy-done.41, f32[1024]{0:T(1024)S(1)} %fusion.86, f32[1024]{0:T(1024)S(1)} %broadcast_multiply_fusion.1, f32[1024]{0:T(1024)S(1)} %get-tuple-element.136, ...), kind=kOutput, calls=%fused_computation.34 | convolution fusion | flops 8598320128 | bytes 25190400 | tf_op jit(solution)/shard_map/tf,df->td/dot_general | solution.py:479
  293.5 33.3 %attention_back.1.y_hbm = bf16[1024,3072]{1,0:T(8,128)(2,1)} custom-call(s32[1024,1]{1,0:T(8,128)S(1)} %copy-done.24, s32[1,1024]{1,0:T(1,128)S(1)} %bitcast.197, bf16[1024,3072]{1,0:T(8,128)(2,1)} %copy-done.34, bf16[1024,3072]{1,0:T(8,128)(2,1)} %copy-done.34, bf16[1024,3072]{1,0:T(8,128)(2,1)} %copy-done.34, ...), custom_call_target="tpu_custom_call" | custom-call | flops 16000000000 | bytes 14680064 | tf_op jit(solution)/shard_map/attention_back/pallas_call | solution.py:365
  329.6 11.2 %grad_qkv_own.1 = (bf16[2,4,64,1536]{3,2,1,0:T(8,128)(2,1)S(1)}, bf16[2,4,64,1536]{3,2,1,0:T(8,128)(2,1)S(1)}) custom-call(s32[4]{0:T(128)S(1)} %pad_add_fusion.refs_0_.coord, f32[1]{0:T(128)} %bitcast.25.scale_ref, bf16[1024,1024]{1,0:T(8,128)(2,1)S(1)} %copy-done.17, bf16[1024,3072]{1,0:T(8,128)(2,1)S(1)} %copy-done.4), custom_call_target="tpu_custom_call" | custom-call | flops 3221225472 | bytes 8388608 | tf_op jit(solution)/shard_map/grad_qkv_own/pallas_call | solution.py:217
  343.1 10.6 %fusion.114 = (f32[1024]{0:T(1024)S(1)}, f32[1024]{0:T(1024)S(1)}, f32[1024,1024]{1,0:T(8,128)}) fusion(f32[1024]{0:T(1024)S(1)} %copy-done.61, f32[1024]{0:T(1024)S(1)} %copy-done.59, bf16[1024,1024]{1,0:T(8,128)(2,1)S(1)} %copy-done.37, bf16[1024,3072]{1,0:T(8,128)(2,1)S(1)} %copy-done.4, bf16[1024,3072]{1,0:T(8,128)(2,1)} %copy-done.26), kind=kOutput, calls=%fused_computation.309 | convolution fusion | flops 6448740352 | bytes 18890752 | tf_op jit(solution)/shard_map/te,de->td/dot_general | solution.py:494
  390.9 10.8 %grad_up_other.1 = (bf16[2,4,64,2048]{3,2,1,0:T(8,128)(2,1)S(1)}, bf16[2,4,64,2048]{3,2,1,0:T(8,128)(2,1)S(1)}) custom-call(s32[4]{0:T(128)S(1)} %pad_add_fusion.refs_0_.coord, f32[1]{0:T(128)} %bitcast.25.scale_ref, bf16[1024,1024]{1,0:T(8,128)(2,1)S(1)} %copy-done.15, bf16[1024,4096]{1,0:T(8,128)(2,1)} %get-tuple-element.45.y_hbm), custom_call_target="tpu_custom_call" | custom-call | flops 4294967296 | bytes 10485760 | tf_op jit(solution)/shard_map/grad_up_other/pallas_call | solution.py:217
  410.5 11.1 %grad_qkv_other.1 = (bf16[2,4,64,1536]{3,2,1,0:T(8,128)(2,1)S(1)}, bf16[2,4,64,1536]{3,2,1,0:T(8,128)(2,1)S(1)}) custom-call(s32[4]{0:T(128)S(1)} %pad_add_fusion.refs_0_.coord, f32[1]{0:T(128)} %bitcast.25.scale_ref, bf16[1024,1024]{1,0:T(8,128)(2,1)S(1)} %copy-done.18, bf16[1024,3072]{1,0:T(8,128)(2,1)S(1)} %copy-done.5), custom_call_target="tpu_custom_call" | custom-call | flops 3221225472 | bytes 8388608 | tf_op jit(solution)/shard_map/grad_qkv_other/pallas_call | solution.py:217
  426.0 13.4 %add_convert_fusion.6 = bf16[1024,1024]{1,0:T(8,128)(2,1)} fusion(f32[1024,1024]{1,0:T(8,128)} %copy-done.40, f32[1024]{0:T(1024)S(1)} %copy-done.69, bf16[1024,4096]{1,0:T(8,128)(2,1)} %get-tuple-element.152.x_hbm, bf16[4096,1024]{1,0:T(8,128)(2,1)S(1)} %bitcast.192), kind=kOutput, calls=%fused_computation.42 | convolution fusion | flops 8593080320 | bytes 23072768 | tf_op jit(solution)/shard_map/dot_general | solution.py:464
  454.4 15.0 %collective-permute-done.37 = bf16[2,4,64,1536]{3,2,1,0:T(8,128)(2,1)S(1)} collective-permute-done((bf16[2,4,64,1536]{3,2,1,0:T(8,128)(2,1)S(1)}, bf16[2,4,64,1536]{3,2,1,0:T(8,128)(2,1)S(1)}, u32[]{:S(2)}, u32[]{:S(2)}) %collective-permute-start.37) | collective-permute-done | bytes 1572896 | tf_op jit(solution)/shard_map/ppermute | solution.py:60
  473.1 18.1 %collective-permute-done.38 = bf16[4,64,1536]{2,1,0:T(8,128)(2,1)S(1)} collective-permute-done((bf16[4,64,1536]{2,1,0:T(8,128)(2,1)S(1)}, bf16[4,64,1536]{2,1,0:T(8,128)(2,1)S(1)}, u32[]{:S(2)}, u32[]{:S(2)}) %collective-permute-start.38) | collective-permute-done | bytes 786464 | tf_op jit(solution)/shard_map/ppermute | solution.py:60
  502.7 20.1 %collective-permute-done.53 = bf16[2,4,64,2048]{3,2,1,0:T(8,128)(2,1)S(1)} collective-permute-done((bf16[2,4,64,2048]{3,2,1,0:T(8,128)(2,1)S(1)}, bf16[2,4,64,2048]{3,2,1,0:T(8,128)(2,1)S(1)}, u32[]{:S(2)}, u32[]{:S(2)}) %collective-permute-start.53) | collective-permute-done | bytes 2097184 | tf_op jit(solution)/shard_map/ppermute | solution.py:60
  530.3 7.6 %collective-permute-done.62 = bf16[4,256,512]{2,1,0:T(8,128)(2,1)} collective-permute-done((bf16[4,256,512]{2,1,0:T(8,128)(2,1)}, bf16[4,256,512]{2,1,0:T(8,128)(2,1)}, u32[]{:S(2)}, u32[]{:S(2)}) %collective-permute-start.62) | collective-permute-done | bytes 1048608 | tf_op jit(solution)/shard_map/ppermute | solution.py:60
  560.4 15.3 %collective-permute-done.64 = bf16[256,512]{1,0:T(8,128)(2,1)S(1)} collective-permute-done((bf16[256,512]{1,0:T(8,128)(2,1)S(1)}, bf16[256,512]{1,0:T(8,128)(2,1)S(1)}, u32[]{:S(2)}, u32[]{:S(2)}) %collective-permute-start.64) | collective-permute-done | bytes 262176 | tf_op jit(solution)/shard_map/ppermute | solution.py:60
  577.0 8.6 %collective-permute-done.56 = bf16[64,2048]{1,0:T(8,128)(2,1)S(1)} collective-permute-done((bf16[64,2048]{1,0:T(8,128)(2,1)S(1)}, bf16[64,2048]{1,0:T(8,128)(2,1)S(1)}, u32[]{:S(2)}, u32[]{:S(2)}) %collective-permute-start.56) | collective-permute-done | bytes 262176 | tf_op jit(solution)/shard_map/ppermute | solution.py:60
  (409 shorter events, 279.3 us)
Async XLA Ops:
  1.5 38.1 %collective-permute-start.2 = (bf16[768]{0:T(1024)(128)(2,1)S(1)}, bf16[768]{0:T(1024)(128)(2,1)S(1)}, u32[]{:S(2)}, u32[]{:S(2)}) collective-permute-start(bf16[768]{0:T(1024)(128)(2,1)S(1)} %convert_element_type.591), channel_id=1, source_target_pairs={{0,12},{1,13},{2,14},{3,15},{4,0},{5,1},{6,2},{7,3},{8,4},{9,5},{1... | collective-permute-start | bytes 4616 | tf_op jit(solution)/shard_map/ppermute | solution.py:60
  6.6 40.0 %collective-permute-start.1 = (bf16[768]{0:T(1024)(128)(2,1)S(1)}, bf16[768]{0:T(1024)(128)(2,1)S(1)}, u32[]{:S(2)}, u32[]{:S(2)}) collective-permute-start(bf16[768]{0:T(1024)(128)(2,1)S(1)} %convert_element_type.591), channel_id=1, source_target_pairs={{0,8},{1,9},{2,10},{3,11},{4,12},{5,13},{6,14},{7,15},{8,0},{9,1},... | collective-permute-start | bytes 4616 | tf_op jit(solution)/shard_map/ppermute | solution.py:60
  28.8 36.4 %collective-permute-start.16 = (bf16[64,2048]{1,0:T(8,128)(2,1)S(1)}, bf16[64,2048]{1,0:T(8,128)(2,1)S(1)}, u32[]{:S(2)}, u32[]{:S(2)}) collective-permute-start(bf16[64,2048]{1,0:T(8,128)(2,1)S(1)} %dynamic-slice_convert_fusion.1), channel_id=1, source_target_pairs={{0,8},{1,9},{2,10},{3,11},{4,12},{5,13},{6,14},{7,15},{8,0},{9,1},... | collective-permute-start | bytes 786440 | tf_op jit(solution)/shard_map/ppermute | solution.py:60
  39.6 35.3 %collective-permute-start.15 = (bf16[64,2048]{1,0:T(8,128)(2,1)S(1)}, bf16[64,2048]{1,0:T(8,128)(2,1)S(1)}, u32[]{:S(2)}, u32[]{:S(2)}) collective-permute-start(bf16[64,2048]{1,0:T(8,128)(2,1)S(1)} %dynamic-slice_convert_fusion.1), channel_id=1, source_target_pairs={{0,4},{1,5},{2,6},{3,7},{4,8},{5,9},{6,10},{7,11},{8,12},{9,13},{1... | collective-permute-start | bytes 786440 | tf_op jit(solution)/shard_map/ppermute | solution.py:60
  48.2 53.7 %collective-permute-start.8 = (bf16[4,64,2048]{2,1,0:T(8,128)(2,1)S(1)}, bf16[4,64,2048]{2,1,0:T(8,128)(2,1)}, u32[]{:S(2)}, u32[]{:S(2)}) collective-permute-start(bf16[4,64,2048]{2,1,0:T(8,128)(2,1)S(1)} %pad_maximum_fusion.refs_1_), channel_id=1, source_target_pairs={{0,2},{1,3},{2,0},{3,1},{4,6},{5,7},{6,4},{7,5},{8,10},{9,11},{10,... | collective-permute-start | bytes 3145736 | tf_op jit(solution)/shard_map/ppermute | solution.py:60
  51.1 50.7 %collective-permute-start.10 = (bf16[4,64,2048]{2,1,0:T(8,128)(2,1)S(1)}, bf16[4,64,2048]{2,1,0:T(8,128)(2,1)}, u32[]{:S(2)}, u32[]{:S(2)}) collective-permute-start(bf16[4,64,2048]{2,1,0:T(8,128)(2,1)S(1)} %collective-permute-done.9.refs_3_), channel_id=1, source_target_pairs={{0,2},{1,3},{2,0},{3,1},{4,6},{5,7},{6,4},{7,5},{8,10},{9,11},{10,... | collective-permute-start | bytes 3145736 | tf_op jit(solution)/shard_map/ppermute | solution.py:60
  114.1 30.2 %collective-permute-start.21 = (bf16[4,64,2048]{2,1,0:T(8,128)(2,1)S(1)}, bf16[4,64,2048]{2,1,0:T(8,128)(2,1)S(1)}, u32[]{:S(2)}, u32[]{:S(2)}) collective-permute-start(bf16[4,64,2048]{2,1,0:T(8,128)(2,1)S(1)} %pad_maximum_fusion.1.refs_1_), channel_id=1, source_target_pairs={{0,16},{16,0},{1,17},{17,1},{2,18},{18,2},{3,19},{19,3},{4,20},{20... | collective-permute-start | bytes 3145736 | tf_op jit(solution)/shard_map/ppermute | solution.py:94
  114.1 30.2 %collective-permute-start.18 = (bf16[4,64,2048]{2,1,0:T(8,128)(2,1)S(1)}, bf16[4,64,2048]{2,1,0:T(8,128)(2,1)S(1)}, u32[]{:S(2)}, u32[]{:S(2)}) collective-permute-start(bf16[4,64,2048]{2,1,0:T(8,128)(2,1)S(1)} %pad_maximum_fusion.1.refs_1_), channel_id=1, source_target_pairs={{0,2},{1,3},{2,0},{3,1},{4,6},{5,7},{6,4},{7,5},{8,10},{9,11},{10,... | collective-permute-start | bytes 3145736 | tf_op jit(solution)/shard_map/ppermute | solution.py:60
  114.6 30.2 %collective-permute-start.29 = (bf16[4,64,2048]{2,1,0:T(8,128)(2,1)S(1)}, bf16[4,64,2048]{2,1,0:T(8,128)(2,1)}, u32[]{:S(2)}, u32[]{:S(2)}) collective-permute-start(bf16[4,64,2048]{2,1,0:T(8,128)(2,1)S(1)} %pad_maximum_fusion.2.refs_1_), channel_id=1, source_target_pairs={{0,1},{1,0},{2,3},{3,2},{4,5},{5,4},{6,7},{7,6},{8,9},{9,8},{10,11... | collective-permute-start | bytes 3145736 | tf_op jit(solution)/shard_map/ppermute | solution.py:60
  116.1 49.1 %collective-permute-start.28 = (bf16[4,64,2048]{2,1,0:T(8,128)(2,1)S(1)}, bf16[4,64,2048]{2,1,0:T(8,128)(2,1)}, u32[]{:S(2)}, u32[]{:S(2)}) collective-permute-start(bf16[4,64,2048]{2,1,0:T(8,128)(2,1)S(1)} %pad_maximum_fusion.2.refs_1_), channel_id=1, source_target_pairs={{0,2},{1,3},{2,0},{3,1},{4,6},{5,7},{6,4},{7,5},{8,10},{9,11},{10,... | collective-permute-start | bytes 3145736 | tf_op jit(solution)/shard_map/ppermute | solution.py:60
  117.6 45.0 %collective-permute-start.20 = (bf16[4,64,2048]{2,1,0:T(8,128)(2,1)}, bf16[4,64,2048]{2,1,0:T(8,128)(2,1)S(1)}, u32[]{:S(2)}, u32[]{:S(2)}) collective-permute-start(bf16[4,64,2048]{2,1,0:T(8,128)(2,1)} %collective-permute-done.19.refs_3_), channel_id=1, source_target_pairs={{0,2},{1,3},{2,0},{3,1},{4,6},{5,7},{6,4},{7,5},{8,10},{9,11},{10,... | collective-permute-start | bytes 3145736 | tf_op jit(solution)/shard_map/ppermute | solution.py:60
  165.3 53.6 %collective-permute-start.31 = (bf16[4,64,2048]{2,1,0:T(8,128)(2,1)S(1)}, bf16[4,64,2048]{2,1,0:T(8,128)(2,1)}, u32[]{:S(2)}, u32[]{:S(2)}) collective-permute-start(bf16[4,64,2048]{2,1,0:T(8,128)(2,1)S(1)} %pad_maximum_fusion.2.refs_1_), channel_id=1, source_target_pairs={{0,16},{16,0},{1,17},{17,1},{2,18},{18,2},{3,19},{19,3},{4,20},{20... | collective-permute-start | bytes 3145736 | tf_op jit(solution)/shard_map/ppermute | solution.py:94
  165.8 53.1 %collective-permute-start.33 = (bf16[4,64,2048]{2,1,0:T(8,128)(2,1)}, bf16[4,64,2048]{2,1,0:T(8,128)(2,1)}, u32[]{:S(2)}, u32[]{:S(2)}) collective-permute-start(bf16[4,64,2048]{2,1,0:T(8,128)(2,1)} %collective-permute-done.29.refs_3_), channel_id=1, source_target_pairs={{0,16},{16,0},{1,17},{17,1},{2,18},{18,2},{3,19},{19,3},{4,20},{20... | collective-permute-start | bytes 3145736 | tf_op jit(solution)/shard_map/ppermute | solution.py:94
  165.8 53.0 %collective-permute-start.32 = (bf16[4,64,2048]{2,1,0:T(8,128)(2,1)}, bf16[4,64,2048]{2,1,0:T(8,128)(2,1)}, u32[]{:S(2)}, u32[]{:S(2)}) collective-permute-start(bf16[4,64,2048]{2,1,0:T(8,128)(2,1)} %collective-permute-done.28.refs_2_), channel_id=1, source_target_pairs={{0,16},{16,0},{1,17},{17,1},{2,18},{18,2},{3,19},{19,3},{4,20},{20... | collective-permute-start | bytes 3145736 | tf_op jit(solution)/shard_map/ppermute | solution.py:94
  173.9 45.0 %collective-permute-start.34 = (bf16[4,64,2048]{2,1,0:T(8,128)(2,1)S(1)}, bf16[4,64,2048]{2,1,0:T(8,128)(2,1)}, u32[]{:S(2)}, u32[]{:S(2)}) collective-permute-start(bf16[4,64,2048]{2,1,0:T(8,128)(2,1)S(1)} %collective-permute-done.30.refs_4_), channel_id=1, source_target_pairs={{0,16},{16,0},{1,17},{17,1},{2,18},{18,2},{3,19},{19,3},{4,20},{20... | collective-permute-start | bytes 3145736 | tf_op jit(solution)/shard_map/ppermute | solution.py:94
  421.7 29.9 %collective-permute-start.60 = (bf16[2,4,256,512]{3,2,1,0:T(8,128)(2,1)S(1)}, bf16[2,4,256,512]{3,2,1,0:T(8,128)(2,1)S(1)}, u32[]{:S(2)}, u32[]{:S(2)}) collective-permute-start(bf16[2,4,256,512]{3,2,1,0:T(8,128)(2,1)S(1)} %copy-done.30), channel_id=1, source_target_pairs={{0,16},{16,0},{1,17},{17,1},{2,18},{18,2},{3,19},{19,3},{4,20},{20... | collective-permute-start | bytes 6291464 | tf_op jit(solution)/shard_map/ppermute | solution.py:241
  421.8 30.5 %collective-permute-start.52 = (bf16[2,4,64,2048]{3,2,1,0:T(8,128)(2,1)}, bf16[2,4,64,2048]{3,2,1,0:T(8,128)(2,1)S(1)}, u32[]{:S(2)}, u32[]{:S(2)}) collective-permute-start(bf16[2,4,64,2048]{3,2,1,0:T(8,128)(2,1)} %copy-done.31), channel_id=1, source_target_pairs={{0,16},{16,0},{1,17},{17,1},{2,18},{18,2},{3,19},{19,3},{4,20},{20... | collective-permute-start | bytes 6291464 | tf_op jit(solution)/shard_map/ppermute | solution.py:241
  451.6 75.2 %collective-permute-start.50 = (bf16[64,512]{1,0:T(8,128)(2,1)S(1)}, bf16[64,512]{1,0:T(8,128)(2,1)S(1)}, u32[]{:S(2)}, u32[]{:S(2)}) collective-permute-start(bf16[64,512]{1,0:T(8,128)(2,1)S(1)} %fusion.78), channel_id=1, source_target_pairs={{0,16},{16,0},{1,17},{17,1},{2,18},{18,2},{3,19},{19,3},{4,20},{20... | collective-permute-start | bytes 196616 | tf_op jit(solution)/shard_map/ppermute | solution.py:519
  452.3 47.9 %collective-permute-start.61 = (bf16[2,4,256,512]{3,2,1,0:T(8,128)(2,1)S(1)}, bf16[2,4,256,512]{3,2,1,0:T(8,128)(2,1)S(1)}, u32[]{:S(2)}, u32[]{:S(2)}) collective-permute-start(bf16[2,4,256,512]{3,2,1,0:T(8,128)(2,1)S(1)} %add_convert_fusion.1), channel_id=1, source_target_pairs={{0,2},{1,3},{2,0},{3,1},{4,6},{5,7},{6,4},{7,5},{8,10},{9,11},{10,... | collective-permute-start | bytes 6291464 | tf_op jit(solution)/shard_map/ppermute | solution.py:60
  469.3 53.4 %collective-permute-start.53 = (bf16[2,4,64,2048]{3,2,1,0:T(8,128)(2,1)S(1)}, bf16[2,4,64,2048]{3,2,1,0:T(8,128)(2,1)S(1)}, u32[]{:S(2)}, u32[]{:S(2)}) collective-permute-start(bf16[2,4,64,2048]{3,2,1,0:T(8,128)(2,1)S(1)} %add_convert_fusion.3), channel_id=1, source_target_pairs={{0,2},{1,3},{2,0},{3,1},{4,6},{5,7},{6,4},{7,5},{8,10},{9,11},{10,... | collective-permute-start | bytes 6291464 | tf_op jit(solution)/shard_map/ppermute | solution.py:60
  491.3 34.3 %collective-permute-start.39 = (bf16[64,1536]{1,0:T(8,128)(2,1)S(1)}, bf16[64,1536]{1,0:T(8,128)(2,1)S(1)}, u32[]{:S(2)}, u32[]{:S(2)}) collective-permute-start(bf16[64,1536]{1,0:T(8,128)(2,1)S(1)} %get-tuple-element.112), channel_id=1, source_target_pairs={{0,4},{1,5},{2,6},{3,7},{4,8},{5,9},{6,10},{7,11},{8,12},{9,13},{1... | collective-permute-start | bytes 589832 | tf_op jit(solution)/shard_map/ppermute | solution.py:60
  491.3 35.2 %collective-permute-start.41 = (bf16[64,1536]{1,0:T(8,128)(2,1)S(1)}, bf16[64,1536]{1,0:T(8,128)(2,1)S(1)}, u32[]{:S(2)}, u32[]{:S(2)}) collective-permute-start(bf16[64,1536]{1,0:T(8,128)(2,1)S(1)} %get-tuple-element.113), channel_id=1, source_target_pairs={{0,12},{1,13},{2,14},{3,15},{4,0},{5,1},{6,2},{7,3},{8,4},{9,5},{1... | collective-permute-start | bytes 589832 | tf_op jit(solution)/shard_map/ppermute | solution.py:60
  543.0 32.7 %collective-permute-start.64 = (bf16[256,512]{1,0:T(8,128)(2,1)S(1)}, bf16[256,512]{1,0:T(8,128)(2,1)S(1)}, u32[]{:S(2)}, u32[]{:S(2)}) collective-permute-start(bf16[256,512]{1,0:T(8,128)(2,1)S(1)} %get-tuple-element.108), channel_id=1, source_target_pairs={{0,8},{1,9},{2,10},{3,11},{4,12},{5,13},{6,14},{7,15},{8,0},{9,1},... | collective-permute-start | bytes 786440 | tf_op jit(solution)/shard_map/ppermute | solution.py:60
  554.3 31.3 %collective-permute-start.56 = (bf16[64,2048]{1,0:T(8,128)(2,1)S(1)}, bf16[64,2048]{1,0:T(8,128)(2,1)S(1)}, u32[]{:S(2)}, u32[]{:S(2)}) collective-permute-start(bf16[64,2048]{1,0:T(8,128)(2,1)S(1)} %get-tuple-element.111), channel_id=1, source_target_pairs={{0,8},{1,9},{2,10},{3,11},{4,12},{5,13},{6,14},{7,15},{8,0},{9,1},... | collective-permute-start | bytes 786440 | tf_op jit(solution)/shard_map/ppermute | solution.py:60
  (128 other events, 1925.2 us)

commit v2 on v1

v2 whole, which is shorter than its diff:
```python
import math

import jax
import jax.numpy as jnp
from jax import lax
from jax.experimental import pallas as pl
from jax.experimental.pallas import tpu as pltpu
from jax.sharding import PartitionSpec as P

HD = 64
STEP = 10
EPS_NORM = 1e-06
CLIP = 1.0
RATE = 0.04
RATE_SMALL = 0.25
DECAY = 0.05
BETA_ONE = 0.9
BETA_TWO = 0.999
EPS_ADAM = 1e-08
F32 = jnp.float32
BF = jnp.bfloat16
BOTH = ("grp", "fsdp")
SWAP = [(0, 1), (1, 0)]
ANY = pl.BlockSpec(memory_space=pl.ANY)
SMEM = pl.BlockSpec(memory_space=pltpu.SMEM)
TILE = 128

RATIO = 0.1


def cost(us):
    return pl.CostEstimate(flops=int(us * RATIO * 1e9), bytes_accessed=0, transcendentals=0)


VMEM = pl.BlockSpec(memory_space=pltpu.VMEM)
SPAN = 256


def dims(n):
    m = max(1, math.isqrt(n // 4))
    return n // (m * m), m


def build_perms(n):
    nz, m = dims(n)

    def chip(z, y, x):
        return (z % nz) * m * m + (y % m) * m + x % m

    def build(move):
        return [
            (c * n + chip(z, y, x), c * n + chip(*move(c, z, y, x)))
            for c in range(2)
            for z in range(nz)
            for y in range(m)
            for x in range(m)
        ]

    return {
        "z": [build(lambda c, z, y, x: (z + k, y, x)) for k in range(nz)],
        "zx": [build(lambda c, z, y, x: (z ^ k, y, x)) for k in range(nz)],
        "a": [build(lambda c, z, y, x: (z, y, x + k) if c == 0 else (z, y + k, x)) for k in range(m)],
        "b": [build(lambda c, z, y, x: (z, y + k, x) if c == 0 else (z, y, x + k)) for k in range(m)],
        "x": [build(lambda c, z, y, x: (z, y, x + k)) for k in range(m)],
        "y": [build(lambda c, z, y, x: (z, y + k, x)) for k in range(m)],
    }


def send(value, table):
    return lax.ppermute(value, BOTH, table)


def layer_norm(x, gain, bias):
    mean = jnp.mean(x, -1, keepdims=True)
    centred = x - mean
    var = jnp.mean(centred * centred, -1, keepdims=True)
    return centred * lax.rsqrt(var + EPS_NORM) * gain + bias


def unpack(small, width, hidden):
    pieces = [small[i * width : (i + 1) * width] for i in range(7)]
    return pieces + [small[7 * width : 7 * width + hidden], small[7 * width + hidden :]]


def adam(weight, first, second, grad, decay, rate):
    first = BETA_ONE * first + (1.0 - BETA_ONE) * grad
    second = BETA_TWO * second + (1.0 - BETA_TWO) * grad * grad
    step_size = (
        first / (1.0 - BETA_ONE**STEP) / (jnp.sqrt(second / (1.0 - BETA_TWO**STEP)) + EPS_ADAM)
    )
    return (weight - rate * (step_size + decay * weight), first, second)


def after(value, *deps):
    return lax.optimization_barrier((value, *deps))[0]


def after_all(values, *deps):
    return lax.optimization_barrier((*values, *deps))[: len(values)]


class Gather:
    def __init__(self, perms, nz, m):
        self.perms, self.nz, self.m = perms, nz, m

    def first(self, start, *hold):
        got = [send(start, self.perms["a"][k]) for k in range(1, self.m)]
        return jnp.stack([after(start, *hold) if hold else start] + got)

    def second(self, part, *deps):
        held = after(part, *deps) if deps else part
        return [part] + [send(held, self.perms["b"][k]) for k in range(1, self.m)]

    def swapped(self, parts, *deps):
        deps = deps or [None] * len(parts)
        first, last = deps[0], deps[-1]
        return [
            lax.ppermute(p if dep is None else after(p, dep), "grp", SWAP)
            for p, dep in zip(parts, [first] + [last] * (len(parts) - 1))
        ]

    def far_start(self, own):
        return jnp.concatenate([own, send(own, self.perms["zx"][1])])

    def far(self, got, deps, hold=()):
        step = 2
        while step < self.nz:
            came = send(after(got, *deps), self.perms["zx"][step])
            got = jnp.concatenate([after(got, *hold) if hold else got, came])
            step *= 2
        return got[1:]

    def sources(self, column, near, near_got, wide, wide_got):
        found = []
        for side, (close, parts) in enumerate(((near, wide), (near_got, wide_got))):
            for ib in range(self.m):
                found.append((close[ib], column, side, [((ia,), 0, ia, ib) for ia in range(self.m)]))
                pieces = [((ia, k - 1), k, ia, ib) for ia in range(self.m) for k in range(1, self.nz)]
                found.append((parts[ib], 0, side, pieces))
        return found


def start_pieces(refs, coord, sources, r, m, put, sems):
    z, y, x, c = coord[0], coord[1], coord[2], coord[3]
    for side in range(2):
        core = c if side == 0 else 1 - c
        for ref, (_, base, at, pieces) in zip(refs, sources):
            if at != side:
                continue
            for index, dz, ia, ib in pieces:
                px = lax.rem(x - jnp.where(core == 0, ia, ib) + m, m)
                py = lax.rem(y - jnp.where(core == 0, ib, ia) + m, m)
                chip = (jnp.bitwise_xor(z, dz) * m + py) * m + px
                src = ref.at[index]
                for dst, scol, cols in put(chip, core):
                    pltpu.make_async_copy(src.at[:, pl.ds(base + scol, cols)], dst, sems.at[side]).start()


def wait_bytes(ref, sem):
    pltpu.make_async_copy(ref, ref, sem).wait()


def aligned_rows(row, r):
    return pl.ds(pl.multiple_of(row, 16), r)


def aligned_cols(col, cols):
    return pl.ds(pl.multiple_of(col, 128), cols)


def pack(coords, qkv, out, up, down, width):
    r = qkv.shape[0]
    quarter, half, wide = width // 4, width // 2, up.shape[1] // 2
    ratio = down.shape[0] // r
    groups = [6 * quarter + half, wide, ratio * half]

    def kernel(coord, q_ref, o_ref, u_ref, d_ref, *outs):
        c = coord[3]

        def store(group, col, value):
            low = value.astype(BF)
            cols = low.shape[1]
            outs[1 + group][0, :, col : col + cols] = low
            at = sum(groups[:group]) + col
            outs[0][0, :, at : at + cols] = low

        for hh in range(2):
            for t in range(3):
                cols = aligned_cols(t * width + hh * half + c * quarter, quarter)
                store(0, (hh * 3 + t) * quarter, q_ref[:, cols])
        store(0, 6 * quarter, o_ref[:, aligned_cols(c * half, half)])
        store(1, 0, u_ref[:, aligned_cols(c * wide, wide)])
        for i in range(ratio):
            store(2, i * half, d_ref[i * r : (i + 1) * r, aligned_cols(c * half, half)])

    return pl.pallas_call(
        kernel,
        out_shape=[jax.ShapeDtypeStruct((1, r, cols), BF) for cols in [sum(groups)] + groups],
        in_specs=[SMEM] + [VMEM] * 4,
        out_specs=[VMEM] * 4,
        compiler_params=pltpu.CompilerParams(vmem_limit_bytes=60 << 20),
        cost_estimate=cost(4),
        name="pack",
    )(coords, qkv, out, up, down)


def assemble(coords, sources, r, m, shape, plan, name):
    def kernel(coord, *refs):
        out, sems = refs[-2:]

        def put(chip, core):
            return [
                (out.at[aligned_rows(row, r), aligned_cols(col, cols)], scol, cols)
                for row, col, cols, scol in plan(chip, core)
            ]

        start_pieces(refs, coord, sources, r, m, put, sems)
        for side in range(2):
            wait_bytes(out.at[:, pl.ds(0, shape[1] // 2)], sems.at[side])

    return pl.pallas_call(
        kernel,
        out_shape=jax.ShapeDtypeStruct(shape, BF),
        in_specs=[SMEM] + [ANY] * len(sources),
        out_specs=pl.BlockSpec(memory_space=pltpu.VMEM),
        scratch_shapes=[pltpu.SemaphoreType.DMA((2,))],
        compiler_params=pltpu.CompilerParams(vmem_limit_bytes=60 << 20),
        cost_estimate=cost(4),
        name=name,
    )(coords, *[source[0] for source in sources])


def project_qkv(coords, sources, normed, bias, r, m):
    rows, width = normed.shape
    part = 3 * width // 4

    def kernel(coord, a_ref, b_ref, *refs):
        out_ref, w_ref, sems = refs[-3:]

        def put(chip, core):
            return [
                (w_ref.at[core, hh, aligned_rows(chip * r, r), :], hh * part, part) for hh in range(2)
            ]

        start_pieces(refs, coord, sources, r, m, put, sems)
        for side in range(2):
            core = coord[3] if side == 0 else 1 - coord[3]
            wait_bytes(w_ref.at[0], sems.at[side])
            for hh in range(2):
                cols = aligned_cols(hh * 2 * part + core * part, part)
                for i in range(0, rows, 256):
                    out = jnp.dot(a_ref[i : i + 256, :], w_ref[core, hh], preferred_element_type=F32)
                    out_ref[i : i + 256, cols] = (out + b_ref[:, cols]).astype(BF)

    vmem = pl.BlockSpec(memory_space=pltpu.VMEM)
    return pl.pallas_call(
        kernel,
        out_shape=jax.ShapeDtypeStruct((rows, 3 * width), BF),
        in_specs=[SMEM, vmem, vmem] + [ANY] * len(sources),
        out_specs=vmem,
        scratch_shapes=[pltpu.VMEM((2, 2, width, part), BF), pltpu.SemaphoreType.DMA((2,))],
        compiler_params=pltpu.CompilerParams(vmem_limit_bytes=60 << 20),
        cost_estimate=cost(10),
        name="project_qkv",
    )(coords, normed, bias.reshape(1, -1), *[source[0] for source in sources])


def project_out(coords, sources, att, tokens, bias, gain_two, bias_two, r, m, first):
    rows, width = att.shape
    half = width // 2

    def kernel(coord, a_ref, t_ref, b_ref, g_ref, c_ref, *refs):
        mid_ref, norm_ref, w_ref, sems = refs[-4:]

        def put(chip, core):
            return [(w_ref.at[aligned_rows(chip * r, r), aligned_cols(core * half, half)], first, half)]

        start_pieces(refs, coord, sources, r, m, put, sems)
        for side in range(2):
            wait_bytes(w_ref.at[:, pl.ds(0, half)], sems.at[side])
        for i in range(0, rows, 128):
            part = slice(i, i + 128)
            mid = (
                t_ref[part, :].astype(F32)
                + jnp.dot(a_ref[part, :], w_ref[...], preferred_element_type=F32)
                + b_ref[...]
            )
            mid_ref[part, :] = mid
            norm_ref[part, :] = layer_norm(mid, g_ref[...], c_ref[...]).astype(BF)

    vmem = pl.BlockSpec(memory_space=pltpu.VMEM)
    return pl.pallas_call(
        kernel,
        out_shape=[
            jax.ShapeDtypeStruct((rows, width), F32),
            jax.ShapeDtypeStruct((rows, width), BF),
            jax.ShapeDtypeStruct((width, width), BF),
        ],
        in_specs=[SMEM] + [vmem] * 5 + [ANY] * len(sources),
        out_specs=[vmem] * 3,
        scratch_shapes=[pltpu.SemaphoreType.DMA((2,))],
        compiler_params=pltpu.CompilerParams(vmem_limit_bytes=60 << 20),
        cost_estimate=cost(8),
        name="project_out",
    )(
        coords, att, tokens, bias.reshape(1, -1), gain_two.reshape(1, -1), bias_two.reshape(1, -1),
        *[source[0] for source in sources],
    )


def weight_grad(coords, scale, pairs, nz, m, name, us):
    tokens, total = pairs[0][0].shape
    halves = [right.shape[1] // 2 for _, right in pairs]
    cols = sum(halves)
    r = total // (nz * m * m)
    zrows = total // nz
    mt = min(256, zrows)
    mc = zrows // mt
    count = len(pairs)

    def kernel(coord, scale_ref, *refs):
        x_hbm = refs[0 : 2 * count : 2]
        y_hbm = refs[1 : 2 * count : 2]
        outs = refs[2 * count : 2 * count + 2]
        scratch = refs[2 * count + 2 :]
        xv = scratch[0:count]
        yv = scratch[count : 2 * count]
        acc, xsem, ysem, osem = scratch[2 * count :]
        z, y, x, c = coord[0], coord[1], coord[2], coord[3]
        weight = scale_ref[0]

        def xcopy(p, dz, i):
            pz = lax.rem(z + dz, nz)
            return pltpu.make_async_copy(
                x_hbm[p].at[:, pl.ds(pl.multiple_of(pz * zrows + i * mt, 128), mt)],
                xv[p].at[dz * mc + i],
                xsem.at[p, dz * mc + i],
            )

        def ycopy(p, side):
            owner = c if side == 0 else 1 - c
            return pltpu.make_async_copy(
                y_hbm[p].at[:, pl.ds(pl.multiple_of(owner * halves[p], 128), halves[p])],
                yv[p].at[side],
                ysem.at[p, side],
            )

        for p in range(count):
            xcopy(p, 0, 0).start()
            ycopy(p, 1).start()
            ycopy(p, 0).start()
        for p in range(count):
            for dz in range(nz):
                for i in range(mc):
                    if dz or i:
                        xcopy(p, dz, i).start()
        copies = []
        for dz in range(nz):
            for i in range(mc):
                for p in range(count):
                    low = sum(halves[:p])
                    xcopy(p, dz, i).wait()
                    left = xv[p][dz * mc + i].T
                    for side in (1, 0):
                        if dz == 0 and i == 0:
                            ycopy(p, side).wait()
                        out = jnp.dot(left, yv[p][side], preferred_element_type=F32)
                        acc[side, dz, i * mt : (i + 1) * mt, low : low + halves[p]] = (
                            out * weight
                        ).astype(BF)
            for side in (1, 0):
                owner = c if side == 0 else 1 - c
                for ib in range(m):
                    for ia in range(m):
                        dx = jnp.where(owner == 0, ia, ib)
                        dy = jnp.where(owner == 0, ib, ia)
                        px = lax.rem(x + dx, m)
                        py = lax.rem(y + dy, m)
                        copy = pltpu.make_async_copy(
                            acc.at[side, dz, pl.ds(pl.multiple_of((py * m + px) * r, 16), r), :],
                            outs[side].at[ib, ia, dz],
                            osem.at[side, dz, ib * m + ia],
                        )
                        copy.start()
                        copies.append(copy)
        for copy in copies:
            copy.wait()

    return pl.pallas_call(
        kernel,
        out_shape=[jax.ShapeDtypeStruct((m, m, nz, r, cols), BF)] * 2,
        in_specs=[SMEM, SMEM] + [ANY] * (2 * count),
        out_specs=[ANY] * 2,
        scratch_shapes=[pltpu.VMEM((nz * mc, tokens, mt), BF) for _ in pairs]
        + [pltpu.VMEM((2, tokens, h), BF) for h in halves]
        + [
            pltpu.VMEM((2, nz, zrows, cols), BF),
            pltpu.SemaphoreType.DMA((count, nz * mc)),
            pltpu.SemaphoreType.DMA((count, 2)),
            pltpu.SemaphoreType.DMA((2, nz, m * m)),
        ],
        compiler_params=pltpu.CompilerParams(vmem_limit_bytes=60 << 20),
        cost_estimate=cost(us),
        name=name,
    )(coords, scale, *[v for pair in pairs for v in pair])


def weight_grad_both(coords, scales, pairs, nz, m, name, us):
    tokens, total = pairs[0][0].shape
    widths = [[own.shape[1] for own, _ in pair[2]] for pair in pairs]
    halves = [sum(w) for w in widths]
    cols = sum(halves)
    r = total // (nz * m * m)
    zrows = total // nz
    count = len(pairs)
    operands, places = [], []
    for pair in pairs:
        places.append(len(operands))
        operands += [*pair[:2], *[v for both in pair[2] for v in both]]

    def kernel(coord, scale_ref, *refs):
        ins = refs[: len(operands)]
        outs = refs[len(operands) : len(operands) + m]
        scratch = refs[len(operands) + m :]
        held = scratch[: 4 * count]
        acc, xsem, ysem, osem = scratch[4 * count :]
        z, y, x, c = coord[0], coord[1], coord[2], coord[3]

        def xcopy(p, who, dz):
            pz = lax.rem(z + dz, nz)
            return pltpu.make_async_copy(
                ins[places[p] + who].at[:, pl.ds(pl.multiple_of(pz * zrows, 128), zrows)],
                held[4 * p + who].at[dz],
                xsem.at[p, who, dz],
            )

        def ycopies(p, who):
            dst = held[4 * p + 2 + who]
            found = []
            for k, h in enumerate(widths[p]):
                at = pl.ds(sum(widths[p][:k]), h)
                src = ins[places[p] + 2 + 2 * k + who]
                found.append(pltpu.make_async_copy(src, dst.at[:, at], ysem.at[p, who, k]))
            return found

        for p in range(count):
            for who in range(2):
                xcopy(p, who, 0).start()
                for copy in ycopies(p, who):
                    copy.start()
        for p in range(count):
            for dz in range(1, nz):
                for who in range(2):
                    xcopy(p, who, dz).start()
        copies = []
        for dz in range(nz):
            for p in range(count):
                low = sum(halves[:p])
                out = None
                for who in range(2):
                    xcopy(p, who, dz).wait()
                    if dz == 0:
                        for copy in ycopies(p, who):
                            copy.wait()
                    part = jnp.dot(
                        held[4 * p + who][dz].T, held[4 * p + 2 + who][...], preferred_element_type=F32
                    )
                    out = part * scale_ref[who] if out is None else out + part * scale_ref[who]
                acc[dz, :, low : low + halves[p]] = out.astype(BF)
            for ib in range(m):
                for ia in range(m):
                    px = lax.rem(x + jnp.where(c == 0, ia, ib), m)
                    py = lax.rem(y + jnp.where(c == 0, ib, ia), m)
                    copy = pltpu.make_async_copy(
                        acc.at[dz, aligned_rows((py * m + px) * r, r), :],
                        outs[ib].at[ia, dz],
                        osem.at[dz, ib * m + ia],
                    )
                    copy.start()
                    copies.append(copy)
        for copy in copies:
            copy.wait()

    shapes = []
    for h in halves:
        shapes += [pltpu.VMEM((nz, tokens, zrows), BF)] * 2 + [pltpu.VMEM((tokens, h), BF)] * 2
    return pl.pallas_call(
        kernel,
        out_shape=[jax.ShapeDtypeStruct((m, nz, r, cols), BF)] * m,
        in_specs=[SMEM, SMEM] + [ANY] * len(operands),
        out_specs=[ANY] * m,
        scratch_shapes=shapes
        + [
            pltpu.VMEM((nz, zrows, cols), BF),
            pltpu.SemaphoreType.DMA((count, 2, nz)),
            pltpu.SemaphoreType.DMA((count, 2, max(len(w) for w in widths))),
            pltpu.SemaphoreType.DMA((nz, m * m)),
        ],
        compiler_params=pltpu.CompilerParams(vmem_limit_bytes=60 << 20),
        cost_estimate=cost(us),
        name=name,
    )(coords, scales, *operands)


def add_parts(keep, got):
    size, cols = keep.shape[0], keep.shape[-1]
    shape = keep.shape[1:]
    flat = math.prod(shape[:-1])
    block = max(16, min(flat, (1 << 19) // (size * cols) // 16 * 16))
    while flat % block:
        block -= 16
    count = len(got) + 1

    def kernel(*refs):
        for k in range(size):
            total = refs[0][k].astype(F32)
            for ref in refs[1:count]:
                total += ref[k].astype(F32)
            refs[count + k][...] = total.astype(BF)

    outs = pl.pallas_call(
        kernel,
        grid=(flat // block,),
        out_shape=[jax.ShapeDtypeStruct((flat, cols), BF)] * size,
        in_specs=[pl.BlockSpec((size, block, cols), lambda i: (0, i, 0))] * count,
        out_specs=[pl.BlockSpec((block, cols), lambda i: (i, 0))] * size,
        compiler_params=pltpu.CompilerParams(vmem_limit_bytes=60 << 20),
        cost_estimate=cost(2),
        name="add_parts",
    )(*[v.reshape(size, flat, cols) for v in [keep, *got]])
    return [out.reshape(shape) for out in outs]


class Reduction:
    def __init__(self, parts, perms, nz, m):
        self.perms, self.sizes = perms, {"b": m, "a": m, "z": nz}
        self.left = ["a", "z"]
        self.pass_on("b", parts)

    def pass_on(self, axis, parts):
        self.keep = parts[0]
        self.got = [send(parts[k], self.perms[axis][k]) for k in range(1, self.sizes[axis])]

    def step(self, *deps):
        if not self.left:
            t = after(self.keep, *deps).astype(F32) if deps else self.keep.astype(F32)
            for part in self.got:
                t = t + part.astype(F32)
            return t
        axis = self.left.pop(0)
        parts = add_parts(after(self.keep, *deps), self.got)
        self.pass_on(axis, parts)
        return parts[-1]


def feed_up(coords, sources, normed, bias, r, m):
    rows, width = normed.shape
    hidden = bias.shape[0]
    half, cols, step = hidden // 2, 512, 256
    tiles = half // cols

    def kernel(coord, a_ref, b_ref, *refs):
        act_ref, slope_ref, w_out, w_ref, sems, osem = refs[-6:]
        j = pl.program_id(0)

        @pl.when(j == 0)
        def _():
            def put(chip, core):
                rows_at = aligned_rows(chip * r, r)
                return [(w_ref.at[core, t, rows_at, :], t * cols, cols) for t in range(tiles)]

            start_pieces(refs, coord, sources, r, m, put, sems)

        for side in range(2):

            @pl.when(j == side * tiles)
            def _():
                wait_bytes(w_ref.at[0], sems.at[side])
                core = coord[3] if side == 0 else 1 - coord[3]
                for t in range(tiles):
                    at = aligned_cols((core * tiles + t) * cols, cols)
                    pltpu.make_async_copy(w_ref.at[core, t], w_out.at[:, at], osem).start()

        @pl.when(j == 2 * tiles - 1)
        def _():
            wait_bytes(w_ref, osem)

        core = jnp.where(j < tiles, coord[3], 1 - coord[3])
        weight = w_ref[core, lax.rem(j, tiles)]
        c0, c1 = math.sqrt(2.0 / math.pi), 0.044715
        for i in range(0, rows, step):
            h = jnp.dot(a_ref[i : i + step, :], weight, preferred_element_type=F32) + b_ref[...]
            square = h * h
            t = jnp.tanh(h * (c0 + (c0 * c1) * square))
            mid = 0.5 * h
            act_ref[i : i + step, :] = (mid + mid * t).astype(BF)
            slope = 0.5 + 0.5 * t + mid * (1.0 - t * t) * (c0 + (3.0 * c0 * c1) * square)
            slope_ref[i : i + step, :] = slope.astype(BF)

    def tile(j, coord):
        return (0, jnp.where(j < tiles, coord[3], 1 - coord[3]) * tiles + lax.rem(j, tiles))

    grid_spec = pltpu.PrefetchScalarGridSpec(
        num_scalar_prefetch=1,
        grid=(2 * tiles,),
        in_specs=[
            pl.BlockSpec((rows, width), lambda j, coord: (0, 0)),
            pl.BlockSpec((1, cols), tile),
        ]
        + [ANY] * len(sources),
        out_specs=[
            pl.BlockSpec((rows, cols), tile),
            pl.BlockSpec((rows, cols), tile),
            ANY,
        ],
        scratch_shapes=[
            pltpu.VMEM((2, tiles, width, cols), BF),
            pltpu.SemaphoreType.DMA((2,)),
            pltpu.SemaphoreType.DMA,
        ],
    )
    return pl.pallas_call(
        kernel,
        grid_spec=grid_spec,
        out_shape=[
            jax.ShapeDtypeStruct((rows, hidden), BF),
            jax.ShapeDtypeStruct((rows, hidden), BF),
            jax.ShapeDtypeStruct((width, hidden), BF),
        ],
        compiler_params=pltpu.CompilerParams(vmem_limit_bytes=60 << 20),
        cost_estimate=cost(25),
        name="feed_up",
    )(coords, normed, bias.reshape(1, hidden), *[source[0] for source in sources])


def feed_back(coords, sources, grad, slope, up, r, m, ratio):
    rows, width = grad.shape
    hidden = up.shape[1]
    half, cols, step = width // 2, 512, 512
    tiles = hidden // cols

    def tile_at(j, coord):
        core = jnp.where(j < tiles // 2, coord[3], 1 - coord[3])
        return core * (tiles // 2) + lax.rem(j, tiles // 2)

    def kernel(coord, g_ref, s_ref, u_ref, *refs):
        mine_ref, other_ref, sum_ref, out_ref, d_out, d_ref, dh_ref, sems, osems = refs[-9:]
        j = pl.program_id(0)

        @pl.when(j == 0)
        def _():
            out_ref[...] = jnp.zeros_like(out_ref)

            def put(chip, core):
                return [
                    (
                        d_ref.at[
                            aligned_rows((chip * ratio + s) * r, r), aligned_cols(core * half, half)
                        ],
                        s * half,
                        half,
                    )
                    for s in range(ratio)
                ]

            start_pieces(refs, coord, sources, r, m, put, sems)
            for side in range(2):
                wait_bytes(d_ref.at[:, pl.ds(0, half)], sems.at[side])
            pltpu.make_async_copy(d_ref, d_out, osems.at[2]).start()

        slot = lax.rem(j, 2)

        @pl.when(j >= 2)
        def _():
            wait_bytes(dh_ref.at[0], osems.at[slot])

        down = d_ref[pl.ds(pl.multiple_of(tile_at(j, coord) * cols, cols), cols), :]
        total = jnp.zeros((1, cols), F32)
        for i in range(0, rows, step):
            part = lax.dot_general(
                g_ref[i : i + step, :], down, (((1,), (1,)), ((), ())), preferred_element_type=F32
            )
            dh = (part * s_ref[i : i + step, :].astype(F32)).astype(BF)
            dh_ref[slot, i : i + step, :] = dh
            total += jnp.sum(dh.astype(F32), 0, keepdims=True)
            out_ref[i : i + step, :] += lax.dot_general(
                dh, u_ref[...], (((1,), (1,)), ((), ())), preferred_element_type=F32
            )
        sum_ref[...] = total

        def copy_out(ref):
            at = aligned_cols(lax.rem(j, tiles // 2) * cols, cols)
            pltpu.make_async_copy(dh_ref.at[slot], ref.at[:, at], osems.at[slot]).start()

        @pl.when(j < tiles // 2)
        def _():
            copy_out(mine_ref)

        @pl.when(j >= tiles // 2)
        def _():
            copy_out(other_ref)

        @pl.when(j == tiles - 1)
        def _():
            for at in range(2):
                wait_bytes(dh_ref.at[0], osems.at[at])
            wait_bytes(d_ref, osems.at[2])

    grid_spec = pltpu.PrefetchScalarGridSpec(
        num_scalar_prefetch=1,
        grid=(tiles,),
        in_specs=[
            pl.BlockSpec((rows, width), lambda j, coord: (0, 0)),
            pl.BlockSpec((rows, cols), lambda j, coord: (0, tile_at(j, coord))),
            pl.BlockSpec((width, cols), lambda j, coord: (0, tile_at(j, coord))),
        ]
        + [ANY] * len(sources),
        out_specs=[
            ANY,
            ANY,
            pl.BlockSpec((1, cols), lambda j, coord: (0, tile_at(j, coord))),
            pl.BlockSpec((rows, width), lambda j, coord: (0, 0)),
            ANY,
        ],
        scratch_shapes=[
            pltpu.VMEM((hidden, width), BF),
            pltpu.VMEM((2, rows, cols), BF),
            pltpu.SemaphoreType.DMA((2,)),
            pltpu.SemaphoreType.DMA((3,)),
        ],
    )
    return pl.pallas_call(
        kernel,
        grid_spec=grid_spec,
        out_shape=[
            jax.ShapeDtypeStruct((rows, hidden // 2), BF),
            jax.ShapeDtypeStruct((rows, hidden // 2), BF),
            jax.ShapeDtypeStruct((1, hidden), F32),
            jax.ShapeDtypeStruct((rows, width), F32),
            jax.ShapeDtypeStruct((hidden, width), BF),
        ],
        compiler_params=pltpu.CompilerParams(vmem_limit_bytes=60 << 20),
        cost_estimate=cost(30),
        name="feed_back",
    )(coords, grad, slope, up, *[source[0] for source in sources])


def norm_back(x, grad, gain):
    mean = jnp.mean(x, -1, keepdims=True)
    centred = x - mean
    inv = lax.rsqrt(jnp.mean(centred * centred, -1, keepdims=True) + EPS_NORM)
    hat = centred * inv
    inner = grad * gain
    back = inv * (
        inner
        - jnp.mean(inner, -1, keepdims=True)
        - hat * jnp.mean(inner * hat, -1, keepdims=True)
    )
    return back, jnp.sum(grad * hat, 0, keepdims=True), jnp.sum(grad, 0, keepdims=True)


def middle_back(coords, cotangent, middle, grad, gain, out):
    rows, width = middle.shape
    block = min(256, rows)

    half = width // 2

    def kernel(coord, c_ref, m_ref, d_ref, g_ref, w_ref, *refs):
        dy_ref, mine_ref, other_ref, a_ref, gain_ref, bias_ref, bo_ref, bd_ref, e_ref = refs

        @pl.when(pl.program_id(0) == 0)
        def _():
            for ref in (gain_ref, bias_ref, bo_ref, bd_ref):
                ref[...] = jnp.zeros_like(ref)

        cot = c_ref[...].astype(F32)
        back, for_gain, for_bias = norm_back(m_ref[...], d_ref[...], g_ref[...])
        dy = cot + back
        low = dy.astype(BF)
        dy_ref[...] = dy
        e_ref[...] = low
        mine_ref[...] = e_ref[:, aligned_cols(coord[3] * half, half)]
        other_ref[...] = e_ref[:, aligned_cols((1 - coord[3]) * half, half)]
        a_ref[...] = lax.dot_general(
            low, w_ref[...], (((1,), (1,)), ((), ())), preferred_element_type=F32
        ).astype(BF)
        gain_ref[...] += for_gain
        bias_ref[...] += for_bias
        bo_ref[...] += jnp.sum(low.astype(F32), 0, keepdims=True)
        bd_ref[...] += jnp.sum(cot, 0, keepdims=True)

    tile = pl.BlockSpec((block, width), lambda i: (i, 0))
    part = pl.BlockSpec((block, half), lambda i: (i, 0))
    line = pl.BlockSpec((1, width), lambda i: (0, 0))
    return pl.pallas_call(
        kernel,
        grid=(rows // block,),
        out_shape=[
            jax.ShapeDtypeStruct((rows, cols), t)
            for cols, t in ((width, F32), (half, BF), (half, BF), (width, BF))
        ]
        + [jax.ShapeDtypeStruct((1, width), F32)] * 4,
        in_specs=[SMEM, tile, tile, tile, line, pl.BlockSpec((width, width), lambda i: (0, 0))],
        out_specs=[tile, part, part, tile] + [line] * 4,
        scratch_shapes=[pltpu.VMEM((block, width), BF)],
        compiler_params=pltpu.CompilerParams(vmem_limit_bytes=60 << 20),
        cost_estimate=cost(7),
        name="middle_back",
    )(coords, cotangent, middle, grad, gain.reshape(1, -1), out)


def input_back(coords, tokens, grad_mid, parts, weight, gain):
    rows, width = tokens.shape
    total = weight.shape[1]
    block = min(256, rows)
    count = len(parts)
    cols = total // count

    def kernel(coord, t_ref, m_ref, w_ref, g_ref, *refs):
        out_ref, gain_ref, bias_ref, sum_ref = refs[count:]

        @pl.when(pl.program_id(0) == 0)
        def _():
            for ref in (gain_ref, bias_ref, sum_ref):
                ref[...] = jnp.zeros_like(ref)

        grad = jnp.zeros((block, width), F32)
        for p in range(count):
            core = coord[3] if p % 2 == 0 else 1 - coord[3]
            part = refs[p][...]
            sum_ref[:, p * cols : (p + 1) * cols] += jnp.sum(part.astype(F32), 0, keepdims=True)
            weight_at = aligned_cols((p // 2 * 2 + core) * cols, cols)
            grad += lax.dot_general(
                part, w_ref[:, weight_at], (((1,), (1,)), ((), ())), preferred_element_type=F32
            )
        back, for_gain, for_bias = norm_back(t_ref[...].astype(F32), grad, g_ref[...])
        out_ref[...] = (m_ref[...] + back).astype(BF)
        gain_ref[...] += for_gain
        bias_ref[...] += for_bias

    tile = pl.BlockSpec((block, width), lambda i: (i, 0))
    line = pl.BlockSpec((1, width), lambda i: (0, 0))
    return pl.pallas_call(
        kernel,
        grid=(rows // block,),
        out_shape=[
            jax.ShapeDtypeStruct((rows, width), BF),
            jax.ShapeDtypeStruct((1, width), F32),
            jax.ShapeDtypeStruct((1, width), F32),
            jax.ShapeDtypeStruct((1, total), F32),
        ],
        in_specs=[SMEM, tile, tile, pl.BlockSpec((width, total), lambda i: (0, 0)), line]
        + [pl.BlockSpec((block, cols), lambda i: (i, 0))] * count,
        out_specs=[tile, line, line, pl.BlockSpec((1, total), lambda i: (0, 0))],
        compiler_params=pltpu.CompilerParams(vmem_limit_bytes=60 << 20),
        cost_estimate=cost(30),
        name="input_back",
    )(coords, tokens, grad_mid, weight, gain.reshape(1, -1), *parts)


def outcome(middle, act, down, bias, before, part, parts):
    rows, width = middle.shape
    hidden = act.shape[1]
    block = 128
    first = part * (rows // parts // block)

    def kernel(m_ref, a_ref, d_ref, b_ref, *refs):
        out = jnp.dot(a_ref[...], d_ref[...], preferred_element_type=F32)
        refs[-1][...] = (m_ref[...] + out + b_ref[...]).astype(BF)

    more = [] if before is None else [before]
    return pl.pallas_call(
        kernel,
        grid=(rows // parts // block,),
        out_shape=jax.ShapeDtypeStruct((rows, width), BF),
        in_specs=[
            pl.BlockSpec((block, width), lambda i: (first + i, 0)),
            pl.BlockSpec((block, hidden), lambda i: (first + i, 0)),
            pl.BlockSpec((hidden, width), lambda i: (0, 0)),
            pl.BlockSpec((1, width), lambda i: (0, 0)),
        ]
        + [ANY] * len(more),
        out_specs=pl.BlockSpec((block, width), lambda i: (first + i, 0)),
        input_output_aliases={4: 0} if more else {},
        compiler_params=pltpu.CompilerParams(vmem_limit_bytes=60 << 20),
        cost_estimate=cost(8),
        name="outcome_" + str(part),
    )(middle, act, down, bias.reshape(1, -1), *more)


def head_stack(block, low_lanes):
    zero = jnp.zeros_like(block)
    return jnp.concatenate(
        [jnp.where(low_lanes, block, zero), jnp.where(low_lanes, zero, block)], 0
    )


def window_block(t, rows):
    return jnp.clip(2 * t - 1, 0, rows // 64 - SPAN // 64)


def window_specs(rows, cols, at=0):
    return [
        pl.BlockSpec((64, cols), lambda t, i=i: (window_block(t, rows) + i, at)) for i in range(SPAN // 64)
    ]


def joined_rows(refs, lanes):
    return jnp.concatenate([ref[:, lanes] for ref in refs], 0)


def attention(project, seg_col, seg_row):
    rows, width = project.shape[0], project.shape[1] // 3
    pairs = width // (2 * HD)
    blocks = SPAN // 64

    def pair_lanes(pair, which):
        hh, rest = divmod(pair, pairs // 2)
        core, within = divmod(rest, pairs // 4)
        quarter = width // 4
        first = (hh * 2 + core) * 3 * quarter + which * quarter + within * 2 * HD
        return slice(first, first + 2 * HD)

    def kernel(row_ref, q_ref, *refs):
        cols, windows, (out_ref, probs_ref) = refs[:blocks], refs[blocks : 2 * blocks], refs[2 * blocks :]
        same = joined_rows(cols, slice(0, 1)) == row_ref[...]
        same = jnp.concatenate([same, same], 1)
        low = lax.broadcasted_iota(jnp.int32, (TILE, 2 * HD), 1) < HD
        for h in range(pairs):
            stack = head_stack(q_ref[:, pair_lanes(h, 0)], low)
            keys = joined_rows(windows, pair_lanes(h, 1))
            scores = lax.dot_general(keys, stack, (((1,), (1,)), ((), ())), preferred_element_type=F32)
            scores = jnp.where(same, scores * HD**-0.5, -1e30)
            expo = jnp.exp(scores - jnp.max(scores, 0, keepdims=True))
            probs = (expo * (1.0 / jnp.sum(expo, 0, keepdims=True))).astype(BF)
            probs_ref[0, h] = probs
            mixed = lax.dot_general(
                probs,
                joined_rows(windows, pair_lanes(h, 2)),
                (((0,), (0,)), ((), ())),
                preferred_element_type=F32,
            )
            out_ref[:, h * 2 * HD : (h + 1) * 2 * HD] = jnp.where(low, mixed[:TILE], mixed[TILE:]).astype(BF)

    return pl.pallas_call(
        kernel,
        grid=(rows // TILE,),
        out_shape=[
            jax.ShapeDtypeStruct((rows, width), BF),
            jax.ShapeDtypeStruct((rows // TILE, pairs, SPAN, 2 * TILE), BF),
        ],
        in_specs=[
            pl.BlockSpec((1, TILE), lambda t: (0, t)),
            pl.BlockSpec((TILE, 3 * width), lambda t: (t, 0)),
        ]
        + window_specs(rows, 1)
        + window_specs(rows, 3 * width),
        out_specs=[
            pl.BlockSpec((TILE, width), lambda t: (t, 0)),
            pl.BlockSpec((1, pairs, SPAN, 2 * TILE), lambda t: (t, 0, 0, 0)),
        ],
        compiler_params=pltpu.CompilerParams(vmem_limit_bytes=60 << 20),
        cost_estimate=cost(14),
        name="attention",
    )(seg_row, project, *[seg_col] * blocks, *[project] * blocks)


def attention_back(coords, project, probs, grad, hh):
    rows, width = project.shape[0], project.shape[1] // 3
    quarter = width // 4
    pairs = width // (2 * HD)
    tiles = rows // TILE
    blocks = SPAN // 64

    def kernel(coord, q_ref, p_ref, g_ref, *refs):
        windows, (mine_ref, other_ref, dk, dv) = refs[:blocks], refs[blocks:]
        t = pl.program_id(0)

        @pl.when(t == 0)
        def _():
            dk[...] = jnp.zeros_like(dk)
            dv[...] = jnp.zeros_like(dv)

        window = pl.ds(pl.multiple_of(window_block(t, rows) * 64, 64), SPAN)
        own = pl.ds(pl.multiple_of(t * TILE, TILE), TILE)
        low = lax.broadcasted_iota(jnp.int32, (TILE, 2 * HD), 1) < HD
        scale = HD**-0.5
        for side, out_ref in enumerate((mine_ref, other_ref)):
            core = coord[3] if side == 0 else 1 - coord[3]
            for within in range(pairs // 4):
                h = within * 2 * HD
                held = slice(side * quarter + h, side * quarter + h + 2 * HD)

                def lanes(which):
                    return aligned_cols(core * 3 * quarter + which * quarter + h, 2 * HD)

                queries = head_stack(q_ref[:, lanes(0)], low)
                grads = head_stack(g_ref[:, aligned_cols(core * quarter + h, 2 * HD)], low)
                soft = p_ref[0, core * (pairs // 4) + within]
                wide = soft.astype(F32)
                grad_probs = lax.dot_general(
                    joined_rows(windows, lanes(2)), grads, (((1,), (1,)), ((), ())),
                    preferred_element_type=F32,
                )
                inner = jnp.sum(wide * grad_probs, 0, keepdims=True)
                grad_scores = (wide * (grad_probs - inner)).astype(BF)
                dv[window, held] += jnp.dot(soft, grads, preferred_element_type=F32)
                dk[window, held] += jnp.dot(grad_scores, queries, preferred_element_type=F32)
                dq = lax.dot_general(
                    grad_scores, joined_rows(windows, lanes(1)), (((0,), (0,)), ((), ())),
                    preferred_element_type=F32,
                )
                out_ref[own, h : h + 2 * HD] = (
                    jnp.where(low, dq[:TILE], dq[TILE:]) * scale
                ).astype(BF)

        @pl.when(t == tiles - 1)
        def _():
            for side, out_ref in enumerate((mine_ref, other_ref)):
                held = slice(side * quarter, (side + 1) * quarter)
                out_ref[:, quarter : 2 * quarter] = (dk[:, held] * scale).astype(BF)
                out_ref[:, 2 * quarter :] = dv[:, held].astype(BF)

    whole = pl.BlockSpec((rows, 3 * quarter), lambda t: (0, 0))
    return pl.pallas_call(
        kernel,
        grid=(tiles,),
        out_shape=[jax.ShapeDtypeStruct((rows, 3 * quarter), BF)] * 2,
        in_specs=[
            SMEM,
            pl.BlockSpec((TILE, 6 * quarter), lambda t: (t, hh)),
            pl.BlockSpec((1, pairs // 2, SPAN, 2 * TILE), lambda t: (t, hh, 0, 0)),
            pl.BlockSpec((TILE, 2 * quarter), lambda t: (t, hh)),
        ]
        + window_specs(rows, 6 * quarter, hh),
        out_specs=[whole, whole],
        scratch_shapes=[pltpu.VMEM((rows, 2 * quarter), F32)] * 2,
        compiler_params=pltpu.CompilerParams(vmem_limit_bytes=60 << 20),
        cost_estimate=cost(16),
        name="attention_back_" + str(hh),
    )(coords, project, probs, grad, *[project] * blocks)


def shards(
    tokens, cotangent, segment_ids, group_counts,
    qkv_weight, out_weight, up_weight, down_weight, small_params,
    qkv_first, out_first, up_first, down_first, small_first,
    qkv_second, out_second, up_second, down_second, small_second,
):
    width = tokens.shape[1]
    hidden = up_weight.shape[1]
    rows = tokens.shape[0]
    n = lax.axis_size("fsdp")
    nz, m = dims(n)
    perms = build_perms(n)
    chip = lax.axis_index("fsdp")
    core = lax.axis_index("grp")
    z, y, x = chip // (m * m), chip // m % m, chip % m
    coords = jnp.stack([z, y, x, core]).astype(jnp.int32)
    r = qkv_weight.shape[0]
    ratio = down_weight.shape[0] // r

    counts = group_counts.astype(F32)
    share = counts / jnp.sum(counts)
    is_local = core >= lax.axis_size("grp") // 2
    mine = jnp.where(is_local, share[1], share[0])
    scales = jnp.stack([mine, jnp.where(is_local, share[0], share[1])])
    scale = mine.reshape(1)
    quarter = width // 4
    hq, ho = 3 * width // 2, width // 2

    gather = Gather(perms, nz, m)
    piece = jnp.broadcast_to(small_params.astype(BF).astype(F32), (2 * n,) + small_params.shape)
    small_full = lax.all_to_all(piece, BOTH, 0, 0, tiled=True)[:n].reshape(-1)
    packed, own_one, own_two, own_three = pack(
        coords, qkv_weight, out_weight, up_weight, down_weight, width
    )
    columns = [0, own_one.shape[2], own_one.shape[2] + own_two.shape[2]]
    near_a = gather.first(packed[0])
    pair_one = gather.far_start(own_one)
    near = gather.second(near_a, pair_one)
    near_got = gather.swapped(near)
    far_one = gather.far(pair_one, ())
    small_full = after(small_full, near_a)
    gain_one, bias_one, bias_query, bias_value, bias_out, gain_two, bias_two, bias_up, bias_down = (
        unpack(small_full, width, hidden)
    )
    normed_one = layer_norm(after(tokens, near_a).astype(F32), gain_one, bias_one).astype(BF)
    qkv_bias = jnp.stack([bias_query, jnp.zeros_like(bias_query), bias_value])
    qkv_bias = qkv_bias.reshape(3, 2, 2, quarter).transpose(1, 2, 0, 3).reshape(-1)
    a_one = gather.first(after(far_one, *near[1:]))
    wide_one = gather.second(a_one, normed_one, qkv_bias)
    one = gather.sources(0, near, near_got, wide_one, gather.swapped(wide_one))
    far_two = gather.far(gather.far_start(after(own_two, pair_one)), (far_one,))
    pair_three = gather.far_start(after(own_three, far_one))

    def exchange(value, *deps):
        return lax.ppermute(after(value, *deps) if deps else value, "grp", SWAP)

    project = project_qkv(coords, one, after(normed_one, far_two, pair_three), qkv_bias, r, m)
    a_two = gather.first(after(far_two, wide_one[-1]), project)
    wide_two = gather.second(a_two, project)
    seg_col, seg_row = segment_ids.reshape(rows, 1), segment_ids.reshape(1, rows)
    att, probs = attention(after(project, a_two), seg_col, seg_row)
    far_three = gather.far(pair_three, (far_two,), (att,))
    middle, normed_two, out_full = project_out(
        coords, one, after(att, far_three), tokens, bias_out, gain_two, bias_two, r, m, hq
    )
    a_three = gather.first(after(far_three, att), middle)
    wide_three = gather.second(a_three, middle)
    two = gather.sources(columns[1], near, near_got, wide_two, gather.swapped(wide_two, project, att))
    got_att = exchange(att)
    act, slope, up_full = feed_up(coords, two, after(normed_two, a_three), bias_up, r, m)
    three = gather.sources(columns[2], near, near_got, wide_three, gather.swapped(wide_three, act))

    got_one = exchange(normed_one, got_att)
    got_two = exchange(normed_two, act)
    own, other = weight_grad(
        coords, scale, [(after(act, got_att, *wide_three[1:]), cotangent)], nz, m, "grad_down", 15
    )
    own_got = exchange(other)
    dh_mine, dh_other, grad_bias_up, grad_normed_two, down_full = feed_back(
        coords, three, after(cotangent, other, got_one), slope, up_full, r, m, ratio
    )
    grad_bias_up = grad_bias_up.reshape(-1)
    dh_got = exchange(dh_other)
    parts = add_parts(after(own, grad_normed_two), [own_got])
    sum_down = Reduction(parts, perms, nz, m)
    (grad_mid, e_mine, e_other, grad_att, *sums) = middle_back(
        coords, cotangent, middle, after(grad_normed_two, parts[-1]), gain_two, out_full
    )
    grad_gain_two, grad_bias_two, grad_bias_out, grad_bias_down = (v.reshape(-1) for v in sums)
    parts = weight_grad_both(
        coords, scales, [(normed_two, got_two, [(after(dh_mine, grad_mid), dh_got)])], nz, m, "grad_up", 14
    )
    sum_up = Reduction(parts, perms, nz, m)
    done = sum_down.step(parts[0])
    grad_att = after(grad_att, done)
    e_got = exchange(e_other, done)
    mine_one, other_one = attention_back(coords, project, probs, grad_att, 0)
    one_got = exchange(other_one)
    done = sum_down.step(mine_one)
    mine_two, other_two = attention_back(coords, project, probs, after(grad_att, done), 1)
    two_got = exchange(other_two)
    done = sum_up.step(mine_two)
    parts = weight_grad_both(
        coords,
        scales,
        [
            (normed_one, got_one, [(after(mine_one, done), one_got), (mine_two, two_got)]),
            (att, got_att, [(e_mine, e_got)]),
        ],
        nz, m, "grad_qkv_out", 16,
    )
    done = sum_up.step(parts[0], *sum_down.got[:2])
    sum_one = Reduction([parts[0]] + [after(part, done) for part in parts[1:]], perms, nz, m)

    qkv_full = assemble(
        after(coords, parts[0], done), one, r, m, (width, 3 * width),
        lambda chip, c: [(chip * r, hh * hq + c * (hq // 2), hq // 2, hh * (hq // 2)) for hh in range(2)],
        "assemble_qkv",
    )
    tokens_grad, *sums = input_back(coords, tokens, grad_mid, [mine_one, other_one, mine_two, other_two], qkv_full, gain_one)
    done = sum_one.step(tokens_grad, *sum_down.got[2:], *sum_up.got[:2])
    sums = after_all(sums, done)
    grad_gain_one, grad_bias_one = sums[0].reshape(-1), sums[1].reshape(-1)
    sums = sums[2].reshape(2, 2, 3, quarter)
    sums = jnp.where(core == 0, sums, sums[:, ::-1]).transpose(2, 0, 1, 3)
    grad_bias_query = sums[0].reshape(-1)
    grad_bias_value = sums[2].reshape(-1)

    grad_small = jnp.concatenate(
        [
            grad_gain_one, grad_bias_one, grad_bias_query, grad_bias_value, grad_bias_out,
            grad_gain_two, grad_bias_two, grad_bias_up, grad_bias_down,
        ]
    )
    grad_small = mine * grad_small.reshape(n, -1)
    grad_small = lax.all_to_all(
        jnp.concatenate([grad_small, grad_small]), BOTH, 0, 0, tiled=True
    )

    top = outcome(middle, after(act, done), down_full, bias_down, None, 0, 2)
    done = sum_one.step(top, *sum_up.got[2:])
    block_output = outcome(middle, act, down_full, bias_down, after(top, done), 1, 2)
    half_down = sum_down.step(block_output)
    half_up = sum_up.step(block_output)
    half_one = sum_one.step(block_output)
    merged_small = jnp.sum(after(grad_small, half_one), 0)
    half_qkv = half_one[:, :hq]
    half_rest = jnp.concatenate([half_up, half_one[:, hq:]], 1)
    hu = hidden // 2

    lows = [piece.astype(BF) for piece in (half_qkv, half_rest, half_down)]
    wide = [piece.astype(F32) for piece in lows]
    small_sq = jnp.where(core == 0, jnp.sum(merged_small * merged_small), 0.0)
    local_sq = sum((jnp.sum(piece * piece) for piece in wide)) + small_sq
    everyone = 2 * n
    shared = lax.all_to_all(jnp.full((everyone, 128), local_sq, F32), BOTH, 0, 0, tiled=True)
    total_sq = jnp.sum(shared[:, 0])
    got = [lax.ppermute(low, "grp", SWAP).astype(F32) for low in lows]

    def joined(i, first, last):
        a, b = wide[i][:, first:last], got[i][:, first:last]
        return jnp.concatenate([jnp.where(core == 0, a, b), jnp.where(core == 0, b, a)], 1)

    def qkv_joined():
        a, b = (v[0].reshape(r, 2, 3, 1, quarter) for v in (wide, got))
        pair = jnp.concatenate([jnp.where(core == 0, a, b), jnp.where(core == 0, b, a)], 3)
        return pair.transpose(0, 2, 1, 3, 4).reshape(r, -1)

    merged = (
        qkv_joined(),
        joined(1, hu, hu + ho),
        joined(1, 0, hu),
        joined(2, 0, ho),
        merged_small,
    )
    clip = jnp.minimum(1.0, CLIP * lax.rsqrt(total_sq))
    olds = (qkv_weight, out_weight, up_weight, down_weight, small_params)
    firsts = (qkv_first, out_first, up_first, down_first, small_first)
    seconds = (qkv_second, out_second, up_second, down_second, small_second)
    decays = (DECAY, DECAY, DECAY, DECAY, 0.0)
    rates = (RATE, RATE, RATE, RATE, RATE_SMALL)
    results = [
        adam(w, f, s, g * clip, dc, rt)
        for w, f, s, g, dc, rt in zip(olds, firsts, seconds, merged, decays, rates)
    ]
    return (
        block_output,
        tokens_grad,
        *[res[0] for res in results],
        *[res[1] for res in results],
        *[res[2] for res in results],
        total_sq,
    )


def solution(mesh):
    token, flat, row, vec = P(BOTH, None), P(BOTH), P("fsdp", None), P("fsdp")
    params = (row, row, row, row, vec)
    return jax.shard_map(
        shards,
        mesh=mesh,
        in_specs=(token, token, flat, P()) + params * 3,
        out_specs=(token, token) + params * 3 + (P(),),
        check_vma=False,
    )
```

time: 627 us -> 489 us (0.78)
  Pallas kernels: 128 us -> 254 us
  matrix products: 97.3 us -> 0 us
  starting transfers between devices: 124 us -> 52.1 us
  waiting for transfers between devices: 163 us -> 91.6 us
  other arithmetic: 64.1 us -> 30.9 us
  blocking collectives: 0 us -> 25 us
  local copies, waits for them, and re-layouts: 36.5 us -> 18.1 us
    pallas_call x13 -> x23, Pallas kernels: 128 us -> 254 us  [the longest x2 33.2 us: weight_grad_both(): pl.pallas_call(kernel, out_shape=[jax.ShapeDtypeStruct((m, nz, r, cols),...]
    dot_general x8 -> x0, matrix products: 97.3 us -> none  [the longest x1 25.7 us: shards(): jnp.einsum('td,fd->tf', after(cotangent, done), down_full, preferred_elem...]
    ppermute x53 -> x29, waiting for transfers between devices: 160 us -> 86 us  [send(): return lax.ppermute(value, BOTH, table)]
    ppermute x53 -> x29, starting transfers between devices: 105 us -> 40.6 us  [send(): return lax.ppermute(value, BOTH, table)]
    all_to_all x0 -> x1, blocking collectives: none -> 25 us  [shards(): small_full = lax.all_to_all(piece, BOTH, 0, 0, tiled=True)[:n].reshape(-1)]
    convert_element_type x25 -> x4, other arithmetic: 26.5 us -> 4.11 us  [the longest x1 2.14 us: shards(): layer_norm(after(tokens, near_a).astype(F32), gain_one, bias_one).astype(BF)]
    unnamed x156 -> x109, local copies, waits for them, and re-layouts: 27.6 us -> 9.19 us
    ppermute x25 -> x19, starting transfers between devices: 19.1 us -> 4.03 us  [the longest x8 1.72 us: swapped(): lax.ppermute(p if dep is None else after(p, dep), 'grp', SWAP)]
  transfers between devices with their start and end apart: 78 -> 50, of which waited for: 24 -> 13; matrix products, arithmetic and copies ran while one was open for 14% -> 6% of each run, Pallas kernels for 10% -> 51%
where the time goes in v2:
time: 489 us; the launch traced here: 479 us
  Pallas kernels  254 us (52%)
  waiting for transfers between devices  91.6 us (19%)
  starting transfers between devices  52.1 us (11%)
  other arithmetic  30.9 us (6%)
  blocking collectives  25 us (5%)
  local copies, waits for them, and re-layouts  18.1 us (4%)
  between operations  7.93 us (2%)
    ppermute x29, waiting for transfers between devices, send(): return lax.ppermute(value, BOTH, table)  86 us
    ppermute x29, starting transfers between devices, send(): return lax.ppermute(value, BOTH, table)  40.6 us
    pallas_call x2, Pallas kernels, weight_grad_both(): pl.pallas_call(kernel, out_shape=[jax.ShapeDtypeStruct((m, nz, r, cols),...  33.2 us
    pallas_call x2, Pallas kernels, attention_back(): pl.pallas_call(kernel, grid=(tiles,), out_shape=[jax.ShapeDtypeStruct((ro...  29.8 us
    pallas_call x1, Pallas kernels, feed_back(): pl.pallas_call(kernel, grid_spec=grid_spec, out_shape=[jax.ShapeDtypeStru...  28.6 us
    pallas_call x1, Pallas kernels, feed_up(): pl.pallas_call(kernel, grid_spec=grid_spec, out_shape=[jax.ShapeDtypeStru...  25.4 us
    all_to_all x1, blocking collectives, shards(): small_full = lax.all_to_all(piece, BOTH, 0, 0, tiled=True)[:n].reshape(-1)  25 us
    pallas_call x7, Pallas kernels, add_parts(): pl.pallas_call(kernel, grid=(flat // block,), out_shape=[jax.ShapeDtypeSt...  23.8 us
  transfers between devices with their start and end apart: 50, of which 13 were waited for; matrix products, arithmetic and copies ran while one was open for 6% of the time, Pallas kernels for 51%

profile of v2, /device:TPU:0, one launch (start us, length us, event | category | flops | bytes accessed | tf_op | source)
XLA Modules:
  0.0 479.2 jit_solution(10303871526203467908)
XLA Ops:
  23.8 25.0 %all_to_all.27 = f32[32,1,768]{2,1,0:T(1,128)S(1)} all-to-all(f32[32,1,768]{2,1,0:T(1,128)S(1)} %broadcast_in_dim.12), channel_id=1, replica_groups=mesh['grp'=2,'fsdp'=16] {'grp','fsdp'}, dimensions={0} | all-to-all | bytes 196608 | tf_op jit(solution)/shard_map/all_to_all | solution.py:1074
  54.2 7.1 %collective-permute-done.7 = bf16[3,64,2048]{2,1,0:T(8,128)(2,1)S(1)} collective-permute-done((bf16[3,64,2048]{2,1,0:T(8,128)(2,1)S(1)}, bf16[3,64,2048]{2,1,0:T(8,128)(2,1)S(1)}, u32[]{:S(2)}, u32[]{:S(2)}) %collective-permute-start.7) | collective-permute-done | bytes 786464 | tf_op jit(solution)/shard_map/ppermute | solution.py:70
  63.9 6.9 %collective-permute-done.2 = bf16[1,64,2048]{2,1,0:T(8,128)(2,1)S(1)} collective-permute-done((bf16[1,64,2048]{2,1,0:T(8,128)(2,1)S(1)}, bf16[1,64,2048]{2,1,0:T(8,128)(2,1)S(1)}, u32[]{:S(2)}, u32[]{:S(2)}) %collective-permute-start.2) | collective-permute-done | bytes 262176 | tf_op jit(solution)/shard_map/ppermute | solution.py:70
  74.2 9.1 %collective-permute-done.8.refs_3_ = bf16[2,3,64,2048]{3,2,1,0:T(8,128)(2,1)} collective-permute-done((bf16[2,3,64,2048]{3,2,1,0:T(8,128)(2,1)}, bf16[2,3,64,2048]{3,2,1,0:T(8,128)(2,1)}, u32[]{:S(2)}, u32[]{:S(2)}) %collective-permute-start.8) | collective-permute-done | bytes 1572896 | tf_op jit(solution)/shard_map/ppermute | solution.py:70
  83.3 12.3 %collective-permute-done.4 = bf16[2,64,2048]{2,1,0:T(8,128)(2,1)S(1)} collective-permute-done((bf16[2,64,2048]{2,1,0:T(8,128)(2,1)S(1)}, bf16[2,64,2048]{2,1,0:T(8,128)(2,1)S(1)}, u32[]{:S(2)}, u32[]{:S(2)}) %collective-permute-start.4) | collective-permute-done | bytes 524320 | tf_op jit(solution)/shard_map/ppermute | solution.py:70
  105.2 13.1 %project_qkv.1.q_ref.refs_4_.refs_5_.refs_6_.refs_7_.refs_0_.refs_1_.refs_2_.refs_3_ = bf16[1024,3072]{1,0:T(8,128)(2,1)} custom-call(s32[4]{0:T(128)} %pad_add_fusion.coord, bf16[1024,1024]{1,0:T(8,128)(2,1)} %fusion.5.a_ref.refs_0_, f32[1,3072]{1,0:T(1,128)} %reshape_reshape.3.b_ref, bf16[2,64,6144]{2,1,0:T(8,128)(2,1)} %copy-done, ...), custom_call_target="tpu_custom_call" | custom-call | flops 1000000000 | tf_op jit(solution)/shard_map/project_qkv/pallas_call | solution.py:256
  125.3 17.0 %attention.1 = (bf16[1024,1024]{1,0:T(8,128)(2,1)}, bf16[8,8,256,256]{3,2,1,0:T(8,128)(2,1)}) custom-call(s32[1,1024]{1,0:T(1,128)} %bitcast.87, bf16[1024,3072]{1,0:T(8,128)(2,1)} %project_qkv.1.q_ref.refs_4_.refs_5_.refs_6_.refs_7_.refs_0_.refs_1_.refs_2_.refs_3_, s32[1024,1]{1,0:T(8,128)} %copy.58.refs_0_.refs_1_.refs_2_.refs_3_, ...), custom_call_target="tpu_custom_call" | custom-call | flops 1400000000 | tf_op jit(solution)/shard_map/attention/pallas_call | solution.py:945
  148.9 10.0 %project_out.1 = (f32[1024,1024]{1,0:T(8,128)}, bf16[1024,1024]{1,0:T(8,128)(2,1)}, bf16[1024,1024]{1,0:T(8,128)(2,1)}) custom-call(s32[4]{0:T(128)} %pad_add_fusion.coord, bf16[1024,1024]{1,0:T(8,128)(2,1)} %get-tuple-element.147.a_ref.refs_6_, bf16[1024,1024]{1,0:T(8,128)(2,1)} %t_ref.3, f32[1,1024]{1,0:T(1,128)} %bitcast.90, f32[1,1024]{1,0:T(1,128)} %bitcast.82, ...), custom_call_target="tpu_custom_call" | custom-call | flops 800000000 | tf_op jit(solution)/shard_map/project_out/pallas_call | solution.py:292
  167.5 25.4 %feed_up.1 = (bf16[1024,4096]{1,0:T(8,128)(2,1)}, bf16[1024,4096]{1,0:T(8,128)(2,1)}, bf16[1024,4096]{1,0:T(8,128)(2,1)}) custom-call(s32[4]{0:T(128)} %pad_add_fusion.coord, bf16[1024,1024]{1,0:T(8,128)(2,1)} %get-tuple-element.175.a_ref.refs_0_, f32[1,4096]{1,0:T(1,128)} %bitcast.80, bf16[2,64,6144]{2,1,0:T(8,128)(2,1)} %copy-done, ...), custom_call_target="tpu_custom_call" | custom-call | flops 2500000000 | tf_op jit(solution)/shard_map/feed_up/pallas_call | solution.py:622
  193.5 17.9 %grad_down.1 = (bf16[2,2,4,256,512]{4,3,2,1,0:T(8,128)(2,1)}, bf16[2,2,4,256,512]{4,3,2,1,0:T(8,128)(2,1)}) custom-call(s32[4]{0:T(128)} %pad_add_fusion.coord, f32[1]{0:T(128)} %bitcast.24.scale_ref, bf16[1024,4096]{1,0:T(8,128)(2,1)} %get-tuple-element.213.refs_0_.a_ref, bf16[1024,1024]{1,0:T(8,128)(2,1)} %c_ref.1), custom_call_target="tpu_custom_call" | custom-call | flops 1500000000 | tf_op jit(solution)/shard_map/grad_down/pallas_call | solution.py:389
  211.9 28.6 %feed_back.1 = (bf16[1024,2048]{1,0:T(8,128)(2,1)}, bf16[1024,2048]{1,0:T(8,128)(2,1)}, f32[1,4096]{1,0:T(1,128)}, f32[1024,1024]{1,0:T(8,128)}, bf16[4096,1024]{1,0:T(8,128)(2,1)}) custom-call(s32[4]{0:T(128)} %pad_add_fusion.coord, bf16[1024,1024]{1,0:T(8,128)(2,1)} %c_ref.1, bf16[1024,4096]{1,0:T(8,128)(2,1)} %get-tuple-element.161.s_ref, ...), custom_call_target="tpu_custom_call" | custom-call | flops 3000000000 | tf_op jit(solution)/shard_map/feed_back/pallas_call | solution.py:732
  241.1 5.9 %add_parts.7 = (bf16[2048,512]{1,0:T(8,128)(2,1)}, bf16[2048,512]{1,0:T(8,128)(2,1)}) custom-call(bf16[2,2048,512]{2,1,0:T(8,128)(2,1)} %bitcast.63, bf16[2,2048,512]{2,1,0:T(8,128)(2,1)} %bitcast.28.refs_1_), custom_call_target="tpu_custom_call" | custom-call | flops 200000000 | tf_op jit(solution)/shard_map/add_parts/pallas_call | solution.py:521
  249.2 10.7 %middle_back.1 = (f32[1024,1024]{1,0:T(8,128)}, bf16[1024,512]{1,0:T(8,128)(2,1)}, bf16[1024,512]{1,0:T(8,128)(2,1)}, bf16[1024,1024]{1,0:T(8,128)(2,1)}, f32[1,...) custom-call(s32[4]{0:T(128)} %pad_add_fusion.coord, bf16[1024,1024]{1,0:T(8,128)(2,1)} %c_ref.1, ...), custom_call_target="tpu_custom_call" | custom-call | flops 700000000 | tf_op jit(solution)/shard_map/middle_back/pallas_call | solution.py:795
  260.0 15.5 %grad_up.1 = (bf16[2,4,64,2048]{3,2,1,0:T(8,128)(2,1)}, bf16[2,4,64,2048]{3,2,1,0:T(8,128)(2,1)}) custom-call(s32[4]{0:T(128)} %pad_add_fusion.coord, f32[2]{0:T(128)} %pad_maximum_fusion.8.scale_ref, bf16[1024,1024]{1,0:T(8,128)(2,1)} %get-tuple-element.175.a_ref.refs_0_, bf16[1024,1024]{1,0:T(8,128)(2,1)} %collective-permute-done.25.refs_1_, ...), custom_call_target="tpu_custom_call" | custom-call | flops 1400000000 | tf_op jit(solution)/shard_map/grad_up/pallas_call | solution.py:487
  282.0 14.9 %attention_back_0.1 = (bf16[1024,768]{1,0:T(8,128)(2,1)}, bf16[1024,768]{1,0:T(8,128)(2,1)}) custom-call(s32[4]{0:T(128)} %pad_add_fusion.coord, bf16[1024,3072]{1,0:T(8,128)(2,1)} %project_qkv.1.q_ref.refs_4_.refs_5_.refs_6_.refs_7_.refs_0_.refs_1_.refs_2_.refs_3_, bf16[8,8,256,256]{3,2,1,0:T(8,128)(2,1)} %get-tuple-element.166.p_ref, ...), custom_call_target="tpu_custom_call" | custom-call | flops 1600000000 | tf_op jit(solution)/shard_map/attention_back_0/pallas_call | solution.py:1025
  296.9 10.2 %collective-permute-done.28.refs_1_ = bf16[4,256,512]{2,1,0:T(8,128)(2,1)} collective-permute-done((bf16[4,256,512]{2,1,0:T(8,128)(2,1)}, bf16[4,256,512]{2,1,0:T(8,128)(2,1)}, u32[]{:S(2)}, u32[]{:S(2)}) %collective-permute-start.28) | collective-permute-done | bytes 1048608 | tf_op jit(solution)/shard_map/ppermute | solution.py:70
  309.6 15.0 %attention_back_1.1 = (bf16[1024,768]{1,0:T(8,128)(2,1)}, bf16[1024,768]{1,0:T(8,128)(2,1)}) custom-call(s32[4]{0:T(128)} %pad_add_fusion.coord, bf16[1024,3072]{1,0:T(8,128)(2,1)} %project_qkv.1.q_ref.refs_4_.refs_5_.refs_6_.refs_7_.refs_0_.refs_1_.refs_2_.refs_3_, bf16[8,8,256,256]{3,2,1,0:T(8,128)(2,1)} %get-tuple-element.166.p_ref, ...), custom_call_target="tpu_custom_call" | custom-call | flops 1600000000 | tf_op jit(solution)/shard_map/attention_back_1/pallas_call | solution.py:1025
  336.6 17.8 %grad_qkv_out.1 = (bf16[2,4,64,2048]{3,2,1,0:T(8,128)(2,1)}, bf16[2,4,64,2048]{3,2,1,0:T(8,128)(2,1)}) custom-call(s32[4]{0:T(128)} %pad_add_fusion.coord, f32[2]{0:T(128)} %pad_maximum_fusion.8.scale_ref, bf16[1024,1024]{1,0:T(8,128)(2,1)} %fusion.5.a_ref.refs_0_, bf16[1024,1024]{1,0:T(8,128)(2,1)} %collective-permute-done.21.refs_1_, ...), custom_call_target="tpu_custom_call" | custom-call | flops 1600000000 | tf_op jit(solution)/shard_map/grad_qkv_out/pallas_call | solution.py:487
  362.1 6.2 %assemble_qkv.1.w_ref = bf16[1024,3072]{1,0:T(8,128)(2,1)} custom-call(s32[4]{0:T(128)} %pad_add_fusion.coord, bf16[2,64,6144]{2,1,0:T(8,128)(2,1)} %copy-done, bf16[2,3,64,2048]{3,2,1,0:T(8,128)(2,1)} %pad_maximum_fusion.1.refs_1_, bf16[2,64,6144]{2,1,0:T(8,128)(2,1)} %copy-done.2, bf16[2,3,64,2048]{3,2,1,0:T(8,128)(2,1)} %collective-permute-done.8.refs_3_, ...), custom_call_target="tpu_custom_call" | custom-call | flops 400000000 | tf_op jit(solution)/shard_map/assemble_qkv/pallas_call | solution.py:221
  368.3 14.7 %input_back.1 = (bf16[1024,1024]{1,0:T(8,128)(2,1)}, f32[1,1024]{1,0:T(1,128)}, f32[1,1024]{1,0:T(1,128)}, f32[1,3072]{1,0:T(1,128)}) custom-call(s32[4]{0:T(128)} %pad_add_fusion.coord, bf16[1024,1024]{1,0:T(8,128)(2,1)} %t_ref.3, f32[1024,1024]{1,0:T(8,128)} %get-tuple-element.177.m_ref, bf16[1024,3072]{1,0:T(8,128)(2,1)} %assemble_qkv.1.w_ref, ...), custom_call_target="tpu_custom_call" | custom-call | flops 3000000000 | tf_op jit(solution)/shard_map/input_back/pallas_call | solution.py:843
  400.1 10.0 %outcome_0.1.refs_0_ = bf16[1024,1024]{1,0:T(8,128)(2,1)} custom-call(f32[1024,1024]{1,0:T(8,128)} %get-tuple-element.148.m_ref, bf16[1024,4096]{1,0:T(8,128)(2,1)} %get-tuple-element.213.refs_0_.a_ref, bf16[4096,1024]{1,0:T(8,128)(2,1)} %get-tuple-element.165.d_ref, f32[1,1024]{1,0:T(1,128)} %bitcast.85), custom_call_target="tpu_custom_call" | custom-call | flops 800000000 | tf_op jit(solution)/shard_map/outcome_0/pallas_call | solution.py:872
  417.4 10.0 %outcome_1.1 = bf16[1024,1024]{1,0:T(8,128)(2,1)} custom-call(f32[1024,1024]{1,0:T(8,128)} %get-tuple-element.148.m_ref, bf16[1024,4096]{1,0:T(8,128)(2,1)} %get-tuple-element.213.refs_0_.a_ref, bf16[4096,1024]{1,0:T(8,128)(2,1)} %get-tuple-element.165.d_ref, f32[1,1024]{1,0:T(1,128)} %bitcast.86, ...), custom_call_target="tpu_custom_call", output_to_operand_aliasing={{}: (4, {})} | custom-call | flops 800000000 | tf_op jit(solution)/shard_map/outcome_1/pallas_call | solution.py:872
  429.4 9.2 %collective-permute-done.42 = bf16[64,2048]{1,0:T(8,128)(2,1)S(1)} collective-permute-done((bf16[64,2048]{1,0:T(8,128)(2,1)}, bf16[64,2048]{1,0:T(8,128)(2,1)S(1)}, u32[]{:S(2)}, u32[]{:S(2)}) %collective-permute-start.42) | collective-permute-done | bytes 262176 | tf_op jit(solution)/shard_map/ppermute | solution.py:70
  438.6 9.0 %collective-permute-done.43 = bf16[64,2048]{1,0:T(8,128)(2,1)S(1)} collective-permute-done((bf16[64,2048]{1,0:T(8,128)(2,1)S(1)}, bf16[64,2048]{1,0:T(8,128)(2,1)S(1)}, u32[]{:S(2)}, u32[]{:S(2)}) %collective-permute-start.43) | collective-permute-done | bytes 262176 | tf_op jit(solution)/shard_map/ppermute | solution.py:70
  (273 shorter events, 149.7 us)
Async XLA Ops:
  19.0 30.2 %collective-permute-start.6 = (bf16[2,64,6144]{2,1,0:T(8,128)(2,1)S(1)}, bf16[2,64,6144]{2,1,0:T(8,128)(2,1)S(1)}, u32[]{:S(2)}, u32[]{:S(2)}) collective-permute-start(bf16[2,64,6144]{2,1,0:T(8,128)(2,1)S(1)} %pad_maximum_fusion.refs_0_), channel_id=1, source_target_pairs={{0,2},{1,3},{2,0},{3,1},{4,6},{5,7},{6,4},{7,5},{8,10},{9,11},{10,... | collective-permute-start | bytes 4718600 | tf_op jit(solution)/shard_map/ppermute | solution.py:70
  21.1 27.7 %collective-permute-start.3 = (bf16[2,64,2048]{2,1,0:T(8,128)(2,1)S(1)}, bf16[2,64,2048]{2,1,0:T(8,128)(2,1)S(1)}, u32[]{:S(2)}, u32[]{:S(2)}) collective-permute-start(bf16[2,64,2048]{2,1,0:T(8,128)(2,1)S(1)} %get-tuple-element.267), channel_id=1, source_target_pairs={{0,8},{1,9},{2,10},{3,11},{4,12},{5,13},{6,14},{7,15},{8,0},{9,1},... | collective-permute-start | bytes 1572872 | tf_op jit(solution)/shard_map/ppermute | solution.py:70
  70.9 24.8 %collective-permute-start.4 = (bf16[2,64,2048]{2,1,0:T(8,128)(2,1)S(1)}, bf16[2,64,2048]{2,1,0:T(8,128)(2,1)S(1)}, u32[]{:S(2)}, u32[]{:S(2)}) collective-permute-start(bf16[2,64,2048]{2,1,0:T(8,128)(2,1)S(1)} %pad_maximum_fusion.5), channel_id=1, source_target_pairs={{0,8},{1,9},{2,10},{3,11},{4,12},{5,13},{6,14},{7,15},{8,0},{9,1},... | collective-permute-start | bytes 1572872 | tf_op jit(solution)/shard_map/ppermute | solution.py:70
  73.6 31.5 %collective-permute-start.9 = (bf16[2,64,6144]{2,1,0:T(8,128)(2,1)S(1)}, bf16[2,64,6144]{2,1,0:T(8,128)(2,1)}, u32[]{:S(2)}, u32[]{:S(2)}) collective-permute-start(bf16[2,64,6144]{2,1,0:T(8,128)(2,1)S(1)} %pad_maximum_fusion.refs_0_), channel_id=1, source_target_pairs={{0,16},{16,0},{1,17},{17,1},{2,18},{18,2},{3,19},{19,3},{4,20},{20... | collective-permute-start | bytes 4718600 | tf_op jit(solution)/shard_map/ppermute | solution.py:118
  73.6 31.5 %collective-permute-start.11 = (bf16[2,64,6144]{2,1,0:T(8,128)(2,1)S(1)}, bf16[2,64,6144]{2,1,0:T(8,128)(2,1)}, u32[]{:S(2)}, u32[]{:S(2)}) collective-permute-start(bf16[2,64,6144]{2,1,0:T(8,128)(2,1)S(1)} %collective-permute-done.6.refs_2_), channel_id=1, source_target_pairs={{0,16},{16,0},{1,17},{17,1},{2,18},{18,2},{3,19},{19,3},{4,20},{20... | collective-permute-start | bytes 4718600 | tf_op jit(solution)/shard_map/ppermute | solution.py:118
  74.1 31.0 %collective-permute-start.10 = (bf16[2,3,64,2048]{3,2,1,0:T(8,128)(2,1)}, bf16[2,3,64,2048]{3,2,1,0:T(8,128)(2,1)}, u32[]{:S(2)}, u32[]{:S(2)}) collective-permute-start(bf16[2,3,64,2048]{3,2,1,0:T(8,128)(2,1)} %pad_maximum_fusion.1.refs_1_), channel_id=1, source_target_pairs={{0,16},{16,0},{1,17},{17,1},{2,18},{18,2},{3,19},{19,3},{4,20},{20... | collective-permute-start | bytes 4718600 | tf_op jit(solution)/shard_map/ppermute | solution.py:118
  121.0 38.0 %collective-permute-start.16 = (bf16[2,3,64,2048]{3,2,1,0:T(8,128)(2,1)}, bf16[2,3,64,2048]{3,2,1,0:T(8,128)(2,1)}, u32[]{:S(2)}, u32[]{:S(2)}) collective-permute-start(bf16[2,3,64,2048]{3,2,1,0:T(8,128)(2,1)} %pad_maximum_fusion.2.refs_1_), channel_id=1, source_target_pairs={{0,2},{1,3},{2,0},{3,1},{4,6},{5,7},{6,4},{7,5},{8,10},{9,11},{10,... | collective-permute-start | bytes 4718600 | tf_op jit(solution)/shard_map/ppermute | solution.py:70
  122.0 25.0 %collective-permute-start.14 = (bf16[2,64,2048]{2,1,0:T(8,128)(2,1)S(1)}, bf16[2,64,2048]{2,1,0:T(8,128)(2,1)S(1)}, u32[]{:S(2)}, u32[]{:S(2)}) collective-permute-start(bf16[2,64,2048]{2,1,0:T(8,128)(2,1)S(1)} %copy-done.12), channel_id=1, source_target_pairs={{0,8},{1,9},{2,10},{3,11},{4,12},{5,13},{6,14},{7,15},{8,0},{9,1},... | collective-permute-start | bytes 1572872 | tf_op jit(solution)/shard_map/ppermute | solution.py:70
  162.0 30.9 %collective-permute-start.20 = (bf16[2,3,64,2048]{3,2,1,0:T(8,128)(2,1)}, bf16[2,3,64,2048]{3,2,1,0:T(8,128)(2,1)}, u32[]{:S(2)}, u32[]{:S(2)}) collective-permute-start(bf16[2,3,64,2048]{3,2,1,0:T(8,128)(2,1)} %pad_maximum_fusion.3.refs_1_), channel_id=1, source_target_pairs={{0,2},{1,3},{2,0},{3,1},{4,6},{5,7},{6,4},{7,5},{8,10},{9,11},{10,... | collective-permute-start | bytes 4718600 | tf_op jit(solution)/shard_map/ppermute | solution.py:70
  164.4 47.6 %collective-permute-start.21 = (bf16[1024,1024]{1,0:T(8,128)(2,1)S(1)}, bf16[1024,1024]{1,0:T(8,128)(2,1)}, u32[]{:S(2)}, u32[]{:S(2)}) collective-permute-start(bf16[1024,1024]{1,0:T(8,128)(2,1)S(1)} %copy-done.3), channel_id=1, source_target_pairs={{0,16},{16,0},{1,17},{17,1},{2,18},{18,2},{3,19},{19,3},{4,20},{20... | collective-permute-start | bytes 6291464 | tf_op jit(solution)/shard_map/ppermute | solution.py:1098
  211.4 29.8 %collective-permute-start.24 = (bf16[2,2,4,256,512]{4,3,2,1,0:T(8,128)(2,1)}, bf16[2,2,4,256,512]{4,3,2,1,0:T(8,128)(2,1)}, u32[]{:S(2)}, u32[]{:S(2)}) collective-permute-start(bf16[2,2,4,256,512]{4,3,2,1,0:T(8,128)(2,1)} %get-tuple-element.158), channel_id=1, source_target_pairs={{0,16},{16,0},{1,17},{17,1},{2,18},{18,2},{3,19},{19,3},{4,20},{20... | collective-permute-start | bytes 12582920 | tf_op jit(solution)/shard_map/ppermute | solution.py:1098
  247.1 30.2 %collective-permute-start.27 = (bf16[2,4,256,512]{3,2,1,0:T(8,128)(2,1)}, bf16[2,4,256,512]{3,2,1,0:T(8,128)(2,1)}, u32[]{:S(2)}, u32[]{:S(2)}) collective-permute-start(bf16[2,4,256,512]{3,2,1,0:T(8,128)(2,1)} %bitcast.102), channel_id=1, source_target_pairs={{0,2},{1,3},{2,0},{3,1},{4,6},{5,7},{6,4},{7,5},{8,10},{9,11},{10,... | collective-permute-start | bytes 6291464 | tf_op jit(solution)/shard_map/ppermute | solution.py:70
  275.5 49.6 %collective-permute-start.29 = (bf16[2,4,64,2048]{3,2,1,0:T(8,128)(2,1)}, bf16[2,4,64,2048]{3,2,1,0:T(8,128)(2,1)S(1)}, u32[]{:S(2)}, u32[]{:S(2)}) collective-permute-start(bf16[2,4,64,2048]{3,2,1,0:T(8,128)(2,1)} %get-tuple-element.191), channel_id=1, source_target_pairs={{0,2},{1,3},{2,0},{3,1},{4,6},{5,7},{6,4},{7,5},{8,10},{9,11},{10,... | collective-permute-start | bytes 6291464 | tf_op jit(solution)/shard_map/ppermute | solution.py:70
  280.6 26.4 %collective-permute-start.28 = (bf16[4,256,512]{2,1,0:T(8,128)(2,1)}, bf16[4,256,512]{2,1,0:T(8,128)(2,1)}, u32[]{:S(2)}, u32[]{:S(2)}) collective-permute-start(bf16[4,256,512]{2,1,0:T(8,128)(2,1)} %bitcast.105), channel_id=1, source_target_pairs={{0,1},{1,0},{2,3},{3,2},{4,5},{5,4},{6,7},{7,6},{8,9},{9,8},{10,11... | collective-permute-start | bytes 3145736 | tf_op jit(solution)/shard_map/ppermute | solution.py:70
  296.9 38.5 %collective-permute-start.30 = (bf16[1024,768]{1,0:T(8,128)(2,1)}, bf16[1024,768]{1,0:T(8,128)(2,1)S(1)}, u32[]{:S(2)}, u32[]{:S(2)}) collective-permute-start(bf16[1024,768]{1,0:T(8,128)(2,1)} %get-tuple-element.194.refs_1_), channel_id=1, source_target_pairs={{0,16},{16,0},{1,17},{17,1},{2,18},{18,2},{3,19},{19,3},{4,20},{20... | collective-permute-start | bytes 4718600 | tf_op jit(solution)/shard_map/ppermute | solution.py:1098
  329.9 24.5 %collective-permute-start.35 = (bf16[4,64,2048]{2,1,0:T(8,128)(2,1)}, bf16[4,64,2048]{2,1,0:T(8,128)(2,1)S(1)}, u32[]{:S(2)}, u32[]{:S(2)}) collective-permute-start(bf16[4,64,2048]{2,1,0:T(8,128)(2,1)} %bitcast.104), channel_id=1, source_target_pairs={{0,1},{1,0},{2,3},{3,2},{4,5},{5,4},{6,7},{7,6},{8,9},{9,8},{10,11... | collective-permute-start | bytes 3145736 | tf_op jit(solution)/shard_map/ppermute | solution.py:70
  331.3 23.0 %collective-permute-start.33 = (bf16[256,512]{1,0:T(8,128)(2,1)}, bf16[256,512]{1,0:T(8,128)(2,1)S(1)}, u32[]{:S(2)}, u32[]{:S(2)}) collective-permute-start(bf16[256,512]{1,0:T(8,128)(2,1)} %get-tuple-element.201), channel_id=1, source_target_pairs={{0,4},{1,5},{2,6},{3,7},{4,8},{5,9},{6,10},{7,11},{8,12},{9,13},{1... | collective-permute-start | bytes 786440 | tf_op jit(solution)/shard_map/ppermute | solution.py:70
  358.0 29.9 %collective-permute-start.39 = (bf16[2,4,64,2048]{3,2,1,0:T(8,128)(2,1)}, bf16[2,4,64,2048]{3,2,1,0:T(8,128)(2,1)S(1)}, u32[]{:S(2)}, u32[]{:S(2)}) collective-permute-start(bf16[2,4,64,2048]{3,2,1,0:T(8,128)(2,1)} %get-tuple-element.211), channel_id=1, source_target_pairs={{0,2},{1,3},{2,0},{3,1},{4,6},{5,7},{6,4},{7,5},{8,10},{9,11},{10,... | collective-permute-start | bytes 6291464 | tf_op jit(solution)/shard_map/ppermute | solution.py:70
  358.3 24.7 %collective-permute-start.36 = (bf16[256,512]{1,0:T(8,128)(2,1)}, bf16[256,512]{1,0:T(8,128)(2,1)S(1)}, u32[]{:S(2)}, u32[]{:S(2)}) collective-permute-start(bf16[256,512]{1,0:T(8,128)(2,1)} %get-tuple-element.187), channel_id=1, source_target_pairs={{0,12},{1,13},{2,14},{3,15},{4,0},{5,1},{6,2},{7,3},{8,4},{9,5},{1... | collective-permute-start | bytes 786440 | tf_op jit(solution)/shard_map/ppermute | solution.py:70
  358.3 51.8 %collective-permute-start.40 = (bf16[64,2048]{1,0:T(8,128)(2,1)}, bf16[64,2048]{1,0:T(8,128)(2,1)S(1)}, u32[]{:S(2)}, u32[]{:S(2)}) collective-permute-start(bf16[64,2048]{1,0:T(8,128)(2,1)} %get-tuple-element.204), channel_id=1, source_target_pairs={{0,12},{1,13},{2,14},{3,15},{4,0},{5,1},{6,2},{7,3},{8,4},{9,5},{1... | collective-permute-start | bytes 786440 | tf_op jit(solution)/shard_map/ppermute | solution.py:70
  359.8 23.2 %collective-permute-start.37 = (bf16[64,2048]{1,0:T(8,128)(2,1)}, bf16[64,2048]{1,0:T(8,128)(2,1)S(1)}, u32[]{:S(2)}, u32[]{:S(2)}) collective-permute-start(bf16[64,2048]{1,0:T(8,128)(2,1)} %get-tuple-element.207), channel_id=1, source_target_pairs={{0,4},{1,5},{2,6},{3,7},{4,8},{5,9},{6,10},{7,11},{8,12},{9,13},{1... | collective-permute-start | bytes 786440 | tf_op jit(solution)/shard_map/ppermute | solution.py:70
  360.4 27.5 %collective-permute-start.38 = (bf16[64,2048]{1,0:T(8,128)(2,1)}, bf16[64,2048]{1,0:T(8,128)(2,1)S(1)}, u32[]{:S(2)}, u32[]{:S(2)}) collective-permute-start(bf16[64,2048]{1,0:T(8,128)(2,1)} %get-tuple-element.208), channel_id=1, source_target_pairs={{0,8},{1,9},{2,10},{3,11},{4,12},{5,13},{6,14},{7,15},{8,0},{9,1},... | collective-permute-start | bytes 786440 | tf_op jit(solution)/shard_map/ppermute | solution.py:70
  413.7 33.9 %collective-permute-start.44 = (bf16[64,2048]{1,0:T(8,128)(2,1)}, bf16[64,2048]{1,0:T(8,128)(2,1)S(1)}, u32[]{:S(2)}, u32[]{:S(2)}) collective-permute-start(bf16[64,2048]{1,0:T(8,128)(2,1)} %get-tuple-element.216), channel_id=1, source_target_pairs={{0,12},{1,13},{2,14},{3,15},{4,0},{5,1},{6,2},{7,3},{8,4},{9,5},{1... | collective-permute-start | bytes 786440 | tf_op jit(solution)/shard_map/ppermute | solution.py:70
  429.2 28.2 %collective-permute-start.47 = (bf16[256,512]{1,0:T(8,128)(2,1)S(1)}, bf16[256,512]{1,0:T(8,128)(2,1)S(1)}, u32[]{:S(2)}, u32[]{:S(2)}) collective-permute-start(bf16[256,512]{1,0:T(8,128)(2,1)S(1)} %get-tuple-element.254), channel_id=1, source_target_pairs={{0,16},{16,0},{1,17},{17,1},{2,18},{18,2},{3,19},{19,3},{4,20},{20... | collective-permute-start | bytes 786440 | tf_op jit(solution)/shard_map/ppermute | solution.py:1201
  (74 other events, 824.1 us)
